TPU v7x, 32 devices: a whole 2x2x4 slice. The times are simulated.
32 devices in a mesh: ctx: 8 (over y, x, core), tp: 4 (over z).
Axes of the slice: x: 2, y: 2, z: 4, core: 2. Of those that a mesh axis runs over, the one named last changes fastest.
Arguments:
- stream: bfloat16 [3072, 8192], P('ctx', 'tp'), may hold values from -40 to 40
- pending: bfloat16 [4, 3072, 8192], P('tp', 'ctx'), may hold values from -5 to 5
- norm_gain: bfloat16 [8192], replicated, may hold values from 0.099609375 to 1.8984375
- w_query: bfloat16 [8192, 4096], P('ctx', 'tp'), may hold values from -0.0625 to 0.0625
- w_key: bfloat16 [8192, 1024], P('ctx'), may hold values from -0.375 to 0.375
- w_value: bfloat16 [8192, 1024], P('ctx'), may hold values from -0.1875 to 0.1875
- w_out: bfloat16 [4096, 8192], P('tp', 'ctx'), may hold values from -0.09375 to 0.09375
- prefix_keys: bfloat16 [8, 6144, 128], P(None, 'ctx'), may hold values from -600 to 600
- prefix_values: bfloat16 [8, 6144, 128], P(None, 'ctx'), may hold values from -6 to 6
- prefix_segments: int32 [6144], P('ctx'), may hold values from 0 to 15, never falling along the last dimension, each value on 1 to 768 neighbouring positions
- stretch_segments: int32 [3072], P('ctx'), may hold values from 0 to 15, never falling along the last dimension, each value on 1 to 384 neighbouring positions
- stretch_offset: int32 [1], replicated, may hold values from 6144 to 12287
Outputs:
- output: bfloat16 [3072, 8192], P('ctx', 'tp')
Inputs may be any that keep to these rules, and one draw needn't show every extreme that they name: `prefix_segments`: never falls along the positions; every trajectory 0 to 15 occurs. `stretch_segments`: never falls along the positions; every trajectory 0 to 15 occurs.
All inputs are finite; a program needn't handle non-finite values.
Results may differ from a plain program's by a relative error of at most 0.024.
Values may be sent and summed in bfloat16 or wider, within the bound.
No kernel may reach another device: no remote copies, remote signals or barrier semaphores. Data moves between devices by JAX's collectives and lax.ppermute only.
A program may use at most 256 MiB of HBM per device.

v0:
```python
import math

import jax
import jax.numpy as jnp
from jax import lax
from jax.sharding import PartitionSpec as P

HQ = 32
KVH = 8
HD = 128


ROPE_BASE = 500000.0
ROPE_FACTOR = 8.0
LOW_FREQ = 1.0
HIGH_FREQ = 4.0
INITIAL_SPAN = 8192.0
NORM_EPSILON = 1e-05
MASKED = -1e30


def inverse_freqs(head_width):
    pair_index = jnp.arange(head_width // 2, dtype=jnp.float32)
    base_freq = ROPE_BASE ** (-2.0 * pair_index / head_width)
    wavelength = 2.0 * math.pi / base_freq
    smooth = (INITIAL_SPAN / wavelength - LOW_FREQ) / (HIGH_FREQ - LOW_FREQ)
    blended = (1.0 - smooth) * base_freq / ROPE_FACTOR + smooth * base_freq
    return jnp.where(
        wavelength < INITIAL_SPAN / HIGH_FREQ,
        base_freq,
        jnp.where(wavelength > INITIAL_SPAN / LOW_FREQ, base_freq / ROPE_FACTOR, blended),
    )


def rotate(vectors, positions):
    head_width = vectors.shape[-1]
    angles = positions[..., None] * inverse_freqs(head_width)
    cosine = jnp.cos(angles)
    sinus = jnp.sin(angles)
    first_half = vectors[..., : head_width // 2]
    second_half = vectors[..., head_width // 2 :]
    return jnp.concatenate(
        [first_half * cosine - second_half * sinus, second_half * cosine + first_half * sinus],
        axis=-1,
    )


def visibility(key_labels, is_prefix, key_pos, query_segs, query_index):
    earlier = key_labels[None, :] <= query_segs[:, None]
    same = (key_labels[None, :] == query_segs[:, None]) & (key_pos[None, :] <= query_index[:, None])
    return jnp.where(is_prefix[None, :], earlier, same)


def update(carry, grouped, key_block, value_block, seen):
    running_max, totals, numerator = carry
    scores = jnp.einsum("hrd,hnd->hrn", grouped, key_block, preferred_element_type=jnp.float32) * (
        1.0 / math.sqrt(HD)
    )
    scores = jnp.where(seen[None], scores, MASKED)
    new_max = jnp.maximum(running_max, jnp.max(scores, axis=2))
    weights = jnp.where(seen[None], jnp.exp(scores - new_max[..., None]), 0.0)
    totals = jnp.sum(weights, axis=2)
    numerator = jnp.einsum(
        "hrn,hnd->hrd",
        weights.astype(jnp.bfloat16),
        value_block,
        preferred_element_type=jnp.float32,
    )
    return (new_max, totals, numerator)


def empty_state(kv_heads, row_count):
    return (
        jnp.full((kv_heads, row_count), MASKED, jnp.float32),
        jnp.zeros((kv_heads, row_count), jnp.float32),
        jnp.zeros((kv_heads, row_count, HD), jnp.float32),
    )


def per_device(
    stream,
    pending,
    norm_gain,
    w_query,
    w_key,
    w_value,
    w_out,
    prefix_keys,
    prefix_values,
    prefix_segments,
    stretch_segments,
    stretch_offset,
):
    tok_rows = stream.shape[0]
    prefix_rows = prefix_keys.shape[1]
    ctx_index = lax.axis_index("ctx")
    tp_index = lax.axis_index("tp")
    gain_wide = norm_gain.astype(jnp.float32)
    whole = lax.all_gather(stream, "tp", axis=1, tiled=True).astype(jnp.float32)
    mean_square = jnp.mean(whole * whole, axis=1, keepdims=True)
    normed = (whole * lax.rsqrt(mean_square + NORM_EPSILON) * gain_wide).astype(jnp.bfloat16)
    q_cols = w_query.shape[1]
    q_heads = q_cols // HD
    full_group = HQ // KVH
    kv_heads = max(1, q_heads // full_group)
    group_size = q_heads // kv_heads
    head_start = tp_index * q_heads // full_group
    kv_cols = kv_heads * HD
    key_slice = lax.dynamic_slice_in_dim(w_key, head_start * HD, kv_cols, 1)
    value_slice = lax.dynamic_slice_in_dim(w_value, head_start * HD, kv_cols, 1)
    pieces = (
        lax.all_gather(w_query, "ctx", axis=0, tiled=True),
        lax.all_gather(key_slice, "ctx", axis=0, tiled=True),
        lax.all_gather(value_slice, "ctx", axis=0, tiled=True),
    )
    query_raw, key_full, value_full = tuple(
        (jnp.dot(normed, piece_rows, preferred_element_type=jnp.float32) for piece_rows in pieces)
    )
    token_index = ctx_index * tok_rows + jnp.arange(tok_rows, dtype=jnp.int32)
    positions = stretch_offset[0].astype(jnp.float32) + token_index.astype(jnp.float32)
    query_rows = rotate(query_raw.reshape(tok_rows, q_heads, HD), positions[:, None]).astype(
        jnp.bfloat16
    )
    new_keys = jnp.transpose(
        rotate(key_full.reshape(tok_rows, kv_heads, HD), positions[:, None]).astype(jnp.bfloat16),
        (1, 0, 2),
    )
    new_values = jnp.transpose(
        value_full.astype(jnp.bfloat16).reshape(tok_rows, kv_heads, HD), (1, 0, 2)
    )
    old_keys = lax.dynamic_slice_in_dim(prefix_keys, head_start, kv_heads, 0)
    old_values = lax.dynamic_slice_in_dim(prefix_values, head_start, kv_heads, 0)
    local_keys = jnp.concatenate([old_keys, new_keys], 1)
    local_values = jnp.concatenate([old_values, new_values], 1)
    key_labels = jnp.concatenate([prefix_segments, stretch_segments])
    key_span = prefix_rows + tok_rows
    grouped = jnp.transpose(
        query_rows.reshape(tok_rows, kv_heads, group_size, HD), (1, 0, 2, 3)
    ).reshape(kv_heads, tok_rows * group_size, HD)
    query_index = jnp.repeat(token_index, group_size)
    query_segs = jnp.repeat(stretch_segments, group_size)
    both = jnp.stack([local_keys, local_values])
    kv_block = lax.all_gather(both, "ctx", axis=2, tiled=True)
    label_block = lax.all_gather(key_labels[None, None, :], "ctx", axis=2, tiled=True)
    key_count = kv_block.shape[2]
    absolute = jnp.arange(key_count, dtype=jnp.int32)
    within = absolute % key_span
    key_pos = absolute // key_span * tok_rows + within - prefix_rows
    seen = visibility(label_block[0, 0], within < prefix_rows, key_pos, query_segs, query_index)
    running_max, totals, numerator = update(
        empty_state(kv_heads, tok_rows * group_size), grouped, kv_block[0], kv_block[1], seen
    )
    attended_heads = (numerator / totals[..., None]).astype(jnp.bfloat16)
    attended = jnp.transpose(
        attended_heads.reshape(kv_heads, tok_rows, group_size, HD), (1, 0, 2, 3)
    ).reshape(tok_rows, q_cols)
    head_terms = jnp.dot(
        attended,
        lax.all_gather(w_out, "ctx", axis=1, tiled=True),
        preferred_element_type=jnp.float32,
    )
    head_share, pending_share = (
        lax.psum_scatter(
            head_terms.astype(jnp.bfloat16), "tp", scatter_dimension=1, tiled=True
        ).astype(jnp.float32),
        lax.psum_scatter(
            pending[0].astype(jnp.float32).astype(jnp.bfloat16),
            "tp",
            scatter_dimension=1,
            tiled=True,
        ).astype(jnp.float32),
    )
    block_share = head_share + pending_share
    return (stream.astype(jnp.float32) + block_share).astype(jnp.bfloat16)


def solution(mesh):
    in_specs = (
        P("ctx", "tp"),
        P("tp", "ctx", None),
        P(),
        P("ctx", "tp"),
        P("ctx", None),
        P("ctx", None),
        P("tp", "ctx"),
        P(None, "ctx", None),
        P(None, "ctx", None),
        P("ctx"),
        P("ctx"),
        P(),
    )
    out_specs = P("ctx", "tp")
    return jax.shard_map(
        per_device, mesh=mesh, in_specs=in_specs, out_specs=out_specs, check_vma=False
    )
```

profile of v0, /device:TPU:0, one launch (start us, length us, event | category | flops | bytes accessed | tf_op | source)
XLA Modules:
  0.0 684.5 jit_solution(1276568617704988951)
XLA Ops:
  7.3 0.8 copy-done
  8.1 0.9 constant_dynamic-slice_fusion.2
  9.1 1.9 constant_dynamic-slice_fusion
  12.3 1.2 constant_dynamic-slice_fusion.1
  14.3 112.8 %all-gather.9.cloned.1.call-done = bf16[384,8192]{1,0:T(8,128)(2,1)} async-done(((bf16[384,2048]{1,0:T(8,128)(2,1)}), bf16[384,8192]{1,0:T(8,128)(2,1)}) %all-gather.9.cloned.1.call-update) | async-done | bytes 6291472 | tf_op jit(solution)/shard_map/all_gather | solution.py:99
  127.0 4.1 fusion.6
  131.1 32.7 %all-gather.13.cloned.1.call-done = bf16[8192,256]{1,0:T(8,128)(2,1)} async-done(((bf16[1024,256]{1,0:T(8,128)(2,1)}), bf16[8192,256]{1,0:T(8,128)(2,1)}) %all-gather.13.cloned.1.call-update) | async-done | bytes 4194320 | tf_op jit(solution)/shard_map/all_gather | solution.py:113
  163.8 6.6 fusion.29
  170.8 31.7 %all-gather.15.cloned.1.call-done = bf16[8192,256]{1,0:T(8,128)(2,1)} async-done(((bf16[1024,256]{1,0:T(8,128)(2,1)}), bf16[8192,256]{1,0:T(8,128)(2,1)}) %all-gather.15.cloned.1.call-update) | async-done | bytes 4194320 | tf_op jit(solution)/shard_map/all_gather | solution.py:114
  202.5 6.6 convolution_convert_fusion.1
  209.6 1.1 pad_maximum_fusion
  212.8 9.2 %all-gather.1 = s32[8,1,1152]{2,1,0:T(1,128)S(1)} all-gather(s32[1,1,1152]{2,1,0:T(1,128)S(1)} %reshape.263), channel_id=2, replica_groups=mesh['ctx'=8,'tp'=4] {'ctx'}, dimensions={0}, use_global_device_ids=true | all-gather | bytes 41472 | tf_op jit(solution)/shard_map/all_gather | solution.py:144
  222.0 19.7 %and_select_fusion = pred[1536,9216]{1,0:T(8,128)(4,1)} fusion(s32[9216]{0:T(1024)S(1)} %bitcast.54, s32[9216]{0:T(1024)S(1)} %fusion.18, s32[1536]{0:T(1024)S(1)} %le.46, s32[1536]{0:T(1024)S(1)} %le.42, pred[9216]{0:T(1024)(128)(4,1)S(1)} %fusion.22), kind=kLoop, calls=%fused_computation.7 | loop fusion | flops 70778880 | bytes 14251008 | tf_op jit(solution)/shard_map/jit(_where)/select_n | solution.py:51
  241.7 52.5 %all-gather.11.cloned.1.call-done = bf16[8192,1024]{1,0:T(8,128)(2,1)} async-done(((bf16[1024,1024]{1,0:T(8,128)(2,1)}), bf16[8192,1024]{1,0:T(8,128)(2,1)}) %all-gather.11.cloned.1.call-update) | async-done | bytes 16777232 | tf_op jit(solution)/shard_map/all_gather | solution.py:112
  294.2 12.1 %convolution_bitcast_fusion = f32[48,8,8,128]{3,1,2,0:T(8,128)S(1)} fusion(bf16[8192,1024]{1,0:T(8,128)(2,1)} %all-gather.11.cloned.1.call-done, bf16[384,8192]{1,0:T(8,128)(2,1)} %all-gather.9.cloned.1.call-done, f32[8192]{0:T(1024)S(1)} %convert_element_type.53, f32[384]{0:T(512)S(1)} %add_rsqrt_fusion), kind=kOutput, calls=%fused_computation.22 | convolution fusion | flops 6455033856 | bytes 24675840 | tf_op jit(solution)/shard_map/dot_general | solution.py:117
  307.3 1.1 pad_maximum_fusion.1
  308.7 46.2 %all-gather.17.cloned.1.call-done = bf16[2,2,9216,128]{3,2,1,0:T(8,128)(2,1)} async-done(((bf16[2,2,1152,128]{3,2,1,0:T(8,128)(2,1)}), bf16[2,2,9216,128]{3,2,1,0:T(8,128)(2,1)}) %all-gather.17.cloned.1.call-update) | async-done | bytes 9437200 | tf_op jit(solution)/shard_map/all_gather | solution.py:143
  354.8 52.1 %fusion = (f32[2,1536]{1,0:T(2,128)S(1)}, f32[2,1536,9216]{2,1,0:T(8,128)}) fusion(pred[1536,9216]{1,0:T(8,128)(4,1)} %and_select_fusion, bf16[2,1536,128]{2,1,0:T(8,128)(2,1)S(1)} %bitcast.50, bf16[2,2,9216,128]{3,2,1,0:T(8,128)(2,1)} %all-gather.17.cloned.1.call-done), kind=kOutput, calls=%fused_computation.2 | convolution fusion | flops 7332688896 | bytes 132919296 | tf_op jit(solution)/shard_map/hrd,hnd->hrn/dot_general | solution.py:56
  407.0 42.7 %fusion.1 = f32[2,1536]{1,0:T(2,128)S(1)} fusion(f32[2,1536,9216]{2,1,0:T(8,128)} %get-tuple-element.14, f32[2,1536]{1,0:T(2,128)S(1)} %broadcast_maximum_fusion, pred[1536,9216]{1,0:T(8,128)(4,1)} %and_select_fusion), kind=kLoop, calls=%fused_computation.3 | loop fusion | flops 141554688 | bytes 127426560 | tf_op jit(solution)/shard_map/reduce_sum | solution.py:62
  449.7 47.7 %fusion.13 = bf16[2,1536,128]{2,1,0:T(8,128)(2,1)S(1)} fusion(bf16[2,2,9216,128]{3,2,1,0:T(8,128)(2,1)} %all-gather.17.cloned.1.call-done, f32[2,1536,9216]{2,1,0:T(8,128)} %get-tuple-element.14, f32[2,1536]{1,0:T(2,128)S(1)} %broadcast_maximum_fusion, pred[1536,9216]{1,0:T(8,128)(4,1)} %and_select_fusion, f32[2,1536]{1,0:T(2,128)S(1)} %fusion.1), kind=kOutput, calls=%fused_computation.19 | convolution fusion | flops 7390101504 | bytes 132931584 | tf_op jit(solution)/shard_map/hrn,hnd->hrd/dot_general | solution.py:63
  498.0 14.6 %convolution_convert_fusion = bf16[384,8192]{1,0:T(8,128)(2,1)} fusion(bf16[384,1024]{0,1:T(8,128)(2,1)S(1)} %bitcast.46, bf16[1024,8192]{1,0:T(8,128)(2,1)} %all-gather.19.cloned.1.call-done), kind=kOutput, calls=%fused_computation.13 | convolution fusion | flops 6445596672 | bytes 23855104 | tf_op jit(solution)/shard_map/dot_general | solution.py:157
  512.6 47.0 %reduce-scatter.5.cloned.1.call-done = bf16[384,2048]{1,0:T(8,128)(2,1)} async-done(((bf16[384,8192]{1,0:T(8,128)(2,1)}), bf16[384,2048]{1,0:T(8,128)(2,1)}) %reduce-scatter.5.cloned.1.call-update) | async-done | bytes 1572880 | tf_op jit(solution)/shard_map/reduce_scatter | solution.py:166
  559.6 113.6 %reduce-scatter.3.cloned.1.call-done = bf16[384,2048]{1,0:T(8,128)(2,1)} async-done(((bf16[384,8192]{1,0:T(8,128)(2,1)}), bf16[384,2048]{1,0:T(8,128)(2,1)}) %reduce-scatter.3.cloned.1.call-update) | async-done | bytes 1572880 | tf_op jit(solution)/shard_map/reduce_scatter | solution.py:163
  673.2 4.4 add_convert_fusion
  (53 shorter events, 6.9 us)
Async XLA Ops:
  6.5 1.6 copy-start
  6.5 5.1 copy-start.2
  6.5 120.5 %all-gather.9.cloned.1.call-start = ((), (), s32[]{:S(2)}) async-start(), calls=%async_computation.2 | async-start | bytes 7864320 | tf_op jit(solution)/shard_map/all_gather | solution.py:99
  7.3 156.6 %all-gather.13.cloned.1.call-start = ((), (), s32[]{:S(2)}) async-start(), calls=%async_computation.4 | async-start | bytes 4718592 | tf_op jit(solution)/shard_map/all_gather | solution.py:113
  9.0 193.5 %all-gather.15.cloned.1.call-start = ((), (), s32[]{:S(2)}) async-start(), calls=%async_computation.5 | async-start | bytes 4718592 | tf_op jit(solution)/shard_map/all_gather | solution.py:114
  11.0 283.3 %all-gather.11.cloned.1.call-start = ((), (), s32[]{:S(2)}) async-start(), calls=%async_computation.3 | async-start | bytes 18874368 | tf_op jit(solution)/shard_map/all_gather | solution.py:112
  11.5 343.3 %all-gather.17.cloned.1.call-start = ((), (), s32[]{:S(2)}) async-start(), calls=%async_computation.6 | async-start | bytes 10616832 | tf_op jit(solution)/shard_map/all_gather | solution.py:143
  209.6 2.9 copy-start.3
  209.6 3.1 copy-start.4
  210.8 287.2 %all-gather.19.cloned.1.call-start = ((), (), s32[]{:S(2)}) async-start(), calls=%async_computation.7 | async-start | bytes 18874368 | tf_op jit(solution)/shard_map/all_gather | solution.py:159
  211.3 348.3 %reduce-scatter.5.cloned.1.call-start = ((), (), s32[]{:S(2)}) async-start(), calls=%async_computation.9 | async-start | bytes 7864320 | tf_op jit(solution)/shard_map/reduce_scatter | solution.py:166
  212.1 461.1 %reduce-scatter.3.cloned.1.call-start = ((), (), s32[]{:S(2)}) async-start(), calls=%async_computation.8 | async-start | bytes 7864320 | tf_op jit(solution)/shard_map/reduce_scatter | solution.py:163
  512.6 165.0 %copy-start.1 = (bf16[1024,1024]{1,0:T(8,128)(2,1)S(1)}, bf16[1024,1024]{1,0:T(8,128)(2,1)}, u32[]{:S(2)}) copy-start(bf16[1024,1024]{1,0:T(8,128)(2,1)} %param.16) | copy-start | bytes 6291460
Sparse Core Ops, SparseCore 0:
  8.9 118.0 all-gather.8
  128.9 34.8 all-gather.12
  165.7 36.7 all-gather.14
  204.2 89.9 all-gather.10
  296.0 58.8 all-gather.16
  356.6 89.8 all-gather.18
  448.8 110.7 reduce-scatter.4
  561.9 111.2 reduce-scatter.2
where the time goes:
time: 685 us; the launch traced here: 684 us
  waiting for transfers between devices  439 us (64%)
  matrix products  140 us (20%)
  other arithmetic  74.9 us (11%)
  between operations  14.4 us (2%)
  blocking collectives  9.23 us (1%)
  local copies, waits for them, and re-layouts  7.01 us (1%)
    reduce_scatter x1, waiting for transfers between devices, per_device(): lax.psum_scatter(head_terms.astype(jnp.bfloat16), 'tp', scatter_dimension...  114 us
    all_gather x1, waiting for transfers between devices, per_device(): whole = lax.all_gather(stream, 'tp', axis=1, tiled=True).astype(jnp.float32)  113 us
    all_gather x1, waiting for transfers between devices, per_device(): lax.all_gather(w_query, 'ctx', axis=0, tiled=True)  52.5 us
    dot_general x1, matrix products, update(): jnp.einsum('hrd,hnd->hrn', grouped, key_block, preferred_element_type=jnp...  52.1 us
    dot_general x1, matrix products, update(): jnp.einsum('hrn,hnd->hrd', weights.astype(jnp.bfloat16), value_block, pre...  47.7 us
    reduce_scatter x1, waiting for transfers between devices, per_device(): lax.psum_scatter(pending[0].astype(jnp.float32).astype(jnp.bfloat16), 'tp...  47 us
    all_gather x1, waiting for transfers between devices, per_device(): kv_block = lax.all_gather(both, 'ctx', axis=2, tiled=True)  46.2 us
    reduce_sum x1, other arithmetic, update(): totals = jnp.sum(weights, axis=2)  42.7 us
  transfers between devices with their start and end apart: 8, of which 7 were waited for; matrix products, arithmetic and copies ran while one was open for 32% of the time, Pallas kernels for 0%

commit v1 on v0

--- a/solution.py
+++ b/solution.py
@@ -1,13 +1,17 @@
+import functools
 import math
 
 import jax
 import jax.numpy as jnp
 from jax import lax
+from jax.experimental import pallas as pl
+from jax.experimental.pallas import tpu as pltpu
 from jax.sharding import PartitionSpec as P
 
 HQ = 32
 KVH = 8
 HD = 128
+NTRAJ = 16
 
 
 ROPE_BASE = 500000.0
@@ -51,13 +55,12 @@
     return jnp.where(is_prefix[None, :], earlier, same)
 
 
-def update(carry, grouped, key_block, value_block, seen):
-    running_max, totals, numerator = carry
+def attend_whole(grouped, key_block, value_block, seen):
     scores = jnp.einsum("hrd,hnd->hrn", grouped, key_block, preferred_element_type=jnp.float32) * (
         1.0 / math.sqrt(HD)
     )
     scores = jnp.where(seen[None], scores, MASKED)
-    new_max = jnp.maximum(running_max, jnp.max(scores, axis=2))
+    new_max = jnp.max(scores, axis=2)
     weights = jnp.where(seen[None], jnp.exp(scores - new_max[..., None]), 0.0)
     totals = jnp.sum(weights, axis=2)
     numerator = jnp.einsum(
@@ -66,18 +69,10 @@
         value_block,
         preferred_element_type=jnp.float32,
     )
-    return (new_max, totals, numerator)
-
-
-def empty_state(kv_heads, row_count):
-    return (
-        jnp.full((kv_heads, row_count), MASKED, jnp.float32),
-        jnp.zeros((kv_heads, row_count), jnp.float32),
-        jnp.zeros((kv_heads, row_count, HD), jnp.float32),
-    )
-
-
-def per_device(
+    return numerator / totals[..., None]
+
+
+def per_device_any(
     stream,
     pending,
     norm_gain,
@@ -147,10 +142,7 @@
     within = absolute % key_span
     key_pos = absolute // key_span * tok_rows + within - prefix_rows
     seen = visibility(label_block[0, 0], within < prefix_rows, key_pos, query_segs, query_index)
-    running_max, totals, numerator = update(
-        empty_state(kv_heads, tok_rows * group_size), grouped, kv_block[0], kv_block[1], seen
-    )
-    attended_heads = (numerator / totals[..., None]).astype(jnp.bfloat16)
+    attended_heads = attend_whole(grouped, kv_block[0], kv_block[1], seen).astype(jnp.bfloat16)
     attended = jnp.transpose(
         attended_heads.reshape(kv_heads, tok_rows, group_size, HD), (1, 0, 2, 3)
     ).reshape(tok_rows, q_cols)
@@ -172,6 +164,478 @@
     )
     block_share = head_share + pending_share
     return (stream.astype(jnp.float32) + block_share).astype(jnp.bfloat16)
+
+
+N_CTX = 8
+N_TP = 4
+VMEM = 56 * 1024 * 1024
+
+
+def swap(x, bit):
+    return lax.ppermute(x, "ctx", [(c, c ^ bit) for c in range(N_CTX)])
+
+
+def line_gather(x, z):
+    def up(v, first):
+        return lax.ppermute(v, "tp", [(i, i + 1) for i in range(first, N_TP - 1)])
+
+    def down(v, first):
+        return lax.ppermute(v, "tp", [(N_TP - 1 - i, N_TP - 2 - i) for i in range(first, N_TP - 1)])
+
+    u1, d1 = up(x, 0), down(x, 0)
+    u2, d2 = up(u1, 1), down(d1, 1)
+    u3, d3 = up(u2, 2), down(d2, 2)
+    low = z < 2
+    a = jnp.where(low, d1, u1)
+    b = jnp.where(low, d2, u2)
+    c = jnp.where(z == 0, d3, jnp.where(z == 1, u1, jnp.where(z == 2, d1, u3)))
+    return (
+        (a, jnp.where(low, z + 1, z - 1)),
+        (b, jnp.where(low, z + 2, z - 2)),
+        (c, jnp.where(z % 2 == 1, 0, 3)),
+    )
+
+
+def plane_gather(block):
+    half = block.shape[0] // 2
+    bx, by = swap(block, 2), swap(block, 4)
+    return block, bx, by, swap(bx[:half], 4), swap(by[half:], 2)
+
+
+def part_maps(steps):
+    q = steps // 4
+
+    def walk(first, count):
+        return lambda i, *_: (jnp.clip(i - first, 0, count - 1), 0)
+
+    return (
+        walk(0, q),
+        walk(q, q),
+        walk(2 * q, q),
+        walk(3 * q, q // 2),
+        walk(3 * q + q // 2, q - q // 2),
+    )
+
+
+def choose(i, steps, refs, use):
+    q = steps // 4
+    edges = (0, q, 2 * q, 3 * q, 3 * q + q // 2, steps)
+    for ref, lo, hi in zip(refs, edges[:-1], edges[1:]):
+
+        @pl.when((i >= lo) & (i < hi))
+        def _():
+            use(ref)
+
+
+def rotated(v, cosine, sinus):
+    return v * cosine + pltpu.roll(v, HD // 2, 1) * sinus
+
+
+def project_kernel(steps, heads, rot_heads, scale, where_ref, x_ref, gain_ref, *rest):
+    weights, (cos_ref, sin_ref, out_ref, acc_ref, square_ref) = rest[:5], rest[5:]
+    i = pl.program_id(0)
+
+    @pl.when(i == 0)
+    def _():
+        acc_ref[...] = jnp.zeros_like(acc_ref)
+        square_ref[...] = jnp.zeros_like(square_ref)
+
+    wide = x_ref[...].astype(jnp.float32)
+    squares = wide * wide
+    total = square_ref[...]
+    for j in range(x_ref.shape[1] // 128):
+        total = total + squares[:, j * 128 : (j + 1) * 128]
+    square_ref[...] = total
+    scaled = (wide * gain_ref[...].astype(jnp.float32)).astype(jnp.bfloat16)
+
+    def use(ref):
+        acc_ref[...] += jnp.dot(scaled, ref[...], preferred_element_type=jnp.float32)
+
+    choose(i, steps, weights, use)
+
+    @pl.when(i == steps - 1)
+    def _():
+        width = x_ref.shape[1] * steps
+        mean = jnp.sum(square_ref[...], axis=1, keepdims=True) * (1.0 / width)
+        factor = lax.rsqrt(mean + NORM_EPSILON)
+        for h in range(heads):
+            v = acc_ref[:, h * HD : (h + 1) * HD] * factor
+            if h < rot_heads:
+                v = rotated(v, cos_ref[...], sin_ref[...]) * scale
+            out_ref[h] = v.astype(jnp.bfloat16)
+
+
+def project(where, x, gain, weights, cosine, sinus, heads, rot_heads, scale):
+    rows, depth = x.shape
+    steps = 16
+    wide = depth // steps
+    cols = heads * HD
+
+    def x_map(i, where_ref):
+        part, sub = i // 4, i % 4
+        chip = where_ref[0] ^ part
+        return (0, chip * 4 + ((sub // 2) ^ where_ref[1]) * 2 + sub % 2)
+
+    maps = part_maps(steps)
+    whole = lambda i, *_: (0, 0)
+    return pl.pallas_call(
+        functools.partial(project_kernel, steps, heads, rot_heads, scale),
+        out_shape=jax.ShapeDtypeStruct((heads, rows, HD), jnp.bfloat16),
+        grid_spec=pltpu.PrefetchScalarGridSpec(
+            num_scalar_prefetch=1,
+            grid=(steps,),
+            in_specs=[
+                pl.BlockSpec((rows, wide), x_map),
+                pl.BlockSpec((1, wide), x_map),
+            ]
+            + [pl.BlockSpec((wide, cols), m) for m in maps]
+            + [pl.BlockSpec((rows, HD), whole), pl.BlockSpec((rows, HD), whole)],
+            out_specs=pl.BlockSpec((heads, rows, HD), lambda i, *_: (0, 0, 0)),
+            scratch_shapes=[
+                pltpu.VMEM((rows, cols), jnp.float32),
+                pltpu.VMEM((rows, 128), jnp.float32),
+            ],
+        ),
+        compiler_params=pltpu.CompilerParams(vmem_limit_bytes=VMEM),
+        cost_estimate=pl.CostEstimate(
+            flops=2 * rows * depth * cols,
+            bytes_accessed=2 * depth * (rows + cols),
+            transcendentals=0,
+        ),
+    )(where, x, gain, *weights, cosine, sinus)
+
+
+BT = 256
+BK = 512
+CHAIN = 2
+
+
+def step(q, k, v_ext, m, acc, hide):
+    s = lax.dot_general(q, k, (((1,), (1,)), ((), ())), preferred_element_type=jnp.float32)
+    if hide is not None:
+        s = hide(s)
+    new = jnp.maximum(m, jnp.max(s, axis=1, keepdims=True))
+    p = jnp.exp2(s - new).astype(jnp.bfloat16)
+    acc = acc * jnp.exp2(m - new) + jnp.dot(p, v_ext, preferred_element_type=jnp.float32)
+    return new, acc
+
+
+def prefix_kernel(bound_ref, q_ref, n_ref, kv_ref, m_out, acc_out, v_ext, m_ref, acc_ref):
+    b = pl.program_id(0)
+    heads, bt = q_ref.shape[0], q_ref.shape[1]
+    rows = CHAIN * bt
+
+    @pl.when(b == 0)
+    def _():
+        v_ext[:, :HD] = kv_ref[1]
+        v_ext[:, HD:] = jnp.ones_like(kv_ref[1])
+
+    m_ref[...] = jnp.full_like(m_ref, MASKED)
+    acc_ref[...] = jnp.zeros_like(acc_ref)
+    n_rows = jnp.concatenate([n_ref[:, :1]] * CHAIN, axis=0)
+
+    def body(kb, masked):
+        start = pl.multiple_of(kb * BK, BK)
+        k = kv_ref[0, pl.ds(start, BK), :]
+        v = v_ext[pl.ds(start, BK), :]
+
+        def hide(s):
+            col = lax.broadcasted_iota(jnp.int32, s.shape, 1) + start
+            return jnp.where(col < n_rows, s, MASKED)
+
+        for g in range(heads // CHAIN):
+            q = q_ref[g * CHAIN : (g + 1) * CHAIN].reshape(rows, HD)
+            new, acc = step(q, k, v, m_ref[g][:, :1], acc_ref[g], hide if masked else None)
+            m_ref[g] = jnp.broadcast_to(new, (rows, 128))
+            acc_ref[g] = acc
+
+    full = bound_ref[0, b] // BK
+    some = (bound_ref[1, b] + BK - 1) // BK
+    lax.fori_loop(0, full, lambda kb, c: (body(kb, False), c)[1], 0)
+    lax.fori_loop(full, some, lambda kb, c: (body(kb, True), c)[1], 0)
+    m_out[0] = m_ref[...]
+    acc_out[0] = acc_ref[...]
+
+
+def attend_prefix(bounds, q, n_tok, kv):
+    heads, tokens, _ = q.shape
+    blocks = tokens // BT
+    chains, rows = heads // CHAIN, CHAIN * BT
+    keys = kv.shape[1]
+    return pl.pallas_call(
+        prefix_kernel,
+        out_shape=(
+            jax.ShapeDtypeStruct((blocks, chains, rows, 128), jnp.float32),
+            jax.ShapeDtypeStruct((blocks, chains, rows, 2 * HD), jnp.float32),
+        ),
+        grid_spec=pltpu.PrefetchScalarGridSpec(
+            num_scalar_prefetch=1,
+            grid=(blocks,),
+            in_specs=[
+                pl.BlockSpec((heads, BT, HD), lambda b, *_: (0, b, 0)),
+                pl.BlockSpec((BT, 128), lambda b, *_: (b, 0)),
+                pl.BlockSpec((2, keys, HD), lambda b, *_: (0, 0, 0)),
+            ],
+            out_specs=(
+                pl.BlockSpec((1, chains, rows, 128), lambda b, *_: (b, 0, 0, 0)),
+                pl.BlockSpec((1, chains, rows, 2 * HD), lambda b, *_: (b, 0, 0, 0)),
+            ),
+            scratch_shapes=[
+                pltpu.VMEM((keys, 2 * HD), jnp.bfloat16),
+                pltpu.VMEM((chains, rows, 128), jnp.float32),
+                pltpu.VMEM((chains, rows, 2 * HD), jnp.float32),
+            ],
+        ),
+        compiler_params=pltpu.CompilerParams(vmem_limit_bytes=VMEM),
+        cost_estimate=pl.CostEstimate(
+            flops=8 * heads * tokens * keys * HD,
+            bytes_accessed=4 * keys * HD,
+            transcendentals=heads * tokens * keys,
+        ),
+    )(bounds, q, n_tok, kv)
+
+
+def new_kernel(halo, q_ref, lo_ref, k_ref, v_ref, m_ref, acc_ref, out_ref):
+    b = pl.program_id(0)
+    heads, bt = q_ref.shape[0], q_ref.shape[1]
+    rows = CHAIN * bt
+    span = halo + bt
+    start = pl.multiple_of(b * bt, bt)
+    k = k_ref[pl.ds(start, span), :]
+    v = v_ref[pl.ds(start, span), :]
+    v_ext = jnp.concatenate([v, jnp.ones_like(v)], axis=1)
+    lo = jnp.concatenate([lo_ref[:, :1]] * CHAIN, axis=0)
+
+    def hide(s):
+        col = lax.broadcasted_iota(jnp.int32, s.shape, 1)
+        row = lax.broadcasted_iota(jnp.int32, s.shape, 0) % bt
+        return jnp.where((col + start >= lo) & (col <= row + halo), s, MASKED)
+
+    for g in range(heads // CHAIN):
+        q = q_ref[g * CHAIN : (g + 1) * CHAIN].reshape(rows, HD)
+        _, acc = step(q, k, v_ext, m_ref[0, g][:, :1], acc_ref[0, g], hide)
+        mixed = (acc[:, :HD] / acc[:, HD:]).astype(jnp.bfloat16)
+        for h in range(CHAIN):
+            at = (g * CHAIN + h) * HD
+            out_ref[:, at : at + HD] = mixed[h * bt : (h + 1) * bt]
+
+
+def attend_new(q, lo_tok, k, v, m, acc):
+    heads, tokens, _ = q.shape
+    blocks = tokens // BT
+    chains, rows = heads // CHAIN, CHAIN * BT
+    halo = k.shape[0] - tokens
+    whole = lambda b: (0, 0)
+    return pl.pallas_call(
+        functools.partial(new_kernel, halo),
+        out_shape=jax.ShapeDtypeStruct((tokens, heads * HD), jnp.bfloat16),
+        grid=(blocks,),
+        in_specs=[
+            pl.BlockSpec((heads, BT, HD), lambda b: (0, b, 0)),
+            pl.BlockSpec((BT, 128), lambda b: (b, 0)),
+            pl.BlockSpec(k.shape, whole),
+            pl.BlockSpec(v.shape, whole),
+            pl.BlockSpec((1, chains, rows, 128), lambda b: (b, 0, 0, 0)),
+            pl.BlockSpec((1, chains, rows, 2 * HD), lambda b: (b, 0, 0, 0)),
+        ],
+        out_specs=pl.BlockSpec((BT, heads * HD), lambda b: (b, 0)),
+        compiler_params=pltpu.CompilerParams(vmem_limit_bytes=VMEM),
+        cost_estimate=pl.CostEstimate(
+            flops=8 * heads * tokens * (halo + BT) * HD,
+            bytes_accessed=4 * tokens * heads * HD * 4,
+            transcendentals=heads * tokens * (halo + BT),
+        ),
+    )(q, lo_tok, k, v, m, acc)
+
+
+def out_kernel(steps, where_ref, x_ref, *rest):
+    weights, (out_ref, acc_ref) = rest[:5], rest[5:]
+    i = pl.program_id(0)
+
+    @pl.when(i == 0)
+    def _():
+        acc_ref[...] = jnp.zeros_like(acc_ref)
+
+    def use(ref):
+        acc_ref[...] += jnp.dot(x_ref[...], ref[...], preferred_element_type=jnp.float32)
+
+    choose(i, steps, weights, use)
+
+    @pl.when(i == steps - 1)
+    def _():
+        out_ref[...] = acc_ref[...].astype(jnp.bfloat16)
+
+
+def out_project(where, x, weights):
+    rows, depth = x.shape
+    cols = weights[0].shape[1]
+    steps = 16
+    wide = depth // steps
+
+    def x_map(i, where_ref):
+        part, sub = i // 4, i % 4
+        return (0, (where_ref[0] ^ part ^ sub) * 4 + sub)
+
+    return pl.pallas_call(
+        functools.partial(out_kernel, steps),
+        out_shape=jax.ShapeDtypeStruct((rows, cols), jnp.bfloat16),
+        grid_spec=pltpu.PrefetchScalarGridSpec(
+            num_scalar_prefetch=1,
+            grid=(steps,),
+            in_specs=[pl.BlockSpec((rows, wide), x_map)]
+            + [pl.BlockSpec((wide, cols), m) for m in part_maps(steps)],
+            out_specs=pl.BlockSpec((rows, cols), lambda i, *_: (0, 0)),
+            scratch_shapes=[pltpu.VMEM((rows, cols), jnp.float32)],
+        ),
+        compiler_params=pltpu.CompilerParams(vmem_limit_bytes=VMEM),
+        cost_estimate=pl.CostEstimate(
+            flops=2 * rows * depth * cols,
+            bytes_accessed=2 * depth * (rows + cols),
+            transcendentals=0,
+        ),
+    )(where, x, *weights)
+
+
+def per_device(
+    stream,
+    pending,
+    norm_gain,
+    w_query,
+    w_key,
+    w_value,
+    w_out,
+    prefix_keys,
+    prefix_values,
+    prefix_segments,
+    stretch_segments,
+    stretch_offset,
+):
+    tok, feat = stream.shape
+    chip_tok = 2 * tok
+    c = lax.axis_index("ctx")
+    z = lax.axis_index("tp")
+    chip, core = c // 2, c % 2
+    where = jnp.stack([chip, core]).astype(jnp.int32)
+    depth = feat * N_TP
+
+    labels = jnp.arange(NTRAJ, dtype=jnp.int32)
+    counts = jnp.stack(
+        [
+            jnp.sum((prefix_segments[:, None] <= labels).astype(jnp.int32), axis=0),
+            jnp.sum((stretch_segments[:, None] < labels).astype(jnp.int32), axis=0),
+        ]
+    )
+    for bit in (1, 2, 4):
+        counts = counts + swap(counts, bit)
+    other_segs = swap(stretch_segments, 1)
+    first = core == 0
+    segs = jnp.concatenate(
+        [
+            jnp.where(first, stretch_segments, other_segs),
+            jnp.where(first, other_segs, stretch_segments),
+        ]
+    )
+    onehot = (segs[:, None] == labels).astype(jnp.int32)
+    n_tok = jnp.sum(onehot * counts[0], axis=1)
+    lo_tok = jnp.sum(onehot * counts[1], axis=1) - chip * chip_tok + tok
+    blocked = n_tok.reshape(chip_tok // BT, BT)
+    bounds = jnp.stack([blocked[:, 0], blocked[:, -1]])
+    n_wide = jnp.broadcast_to(n_tok[:, None], (chip_tok, 128))
+    lo_wide = jnp.broadcast_to(lo_tok[:, None], (chip_tok, 128))
+
+    token_index = chip * chip_tok + jnp.arange(chip_tok, dtype=jnp.int32)
+    positions = stretch_offset[0].astype(jnp.float32) + token_index.astype(jnp.float32)
+    angles = positions[:, None] * inverse_freqs(HD)
+    cosine, sinus = jnp.cos(angles), jnp.sin(angles)
+    cosine = jnp.concatenate([cosine, cosine], axis=1)
+    sinus = jnp.concatenate([-sinus, sinus], axis=1)
+
+    def columns(w, width, base):
+        mine = lax.dynamic_slice_in_dim(w, base + core * width, width, 1)
+        theirs = lax.dynamic_slice_in_dim(w, base + (1 - core) * width, width, 1)
+        return mine, theirs
+
+    def chip_block(mine, theirs):
+        return jnp.concatenate([mine, swap(theirs, 1)], axis=0)
+
+    q_heads = w_query.shape[1] // HD // 2
+    kv_old = jnp.stack([prefix_keys, prefix_values])
+    mine_old = lax.dynamic_index_in_dim(kv_old, 2 * z + core, 1, keepdims=False)
+    theirs_old = swap(lax.dynamic_index_in_dim(kv_old, 2 * z + 1 - core, 1, keepdims=False), 1)
+    old = jnp.where(
+        first,
+        jnp.concatenate([mine_old, theirs_old], axis=1),
+        jnp.concatenate([theirs_old, mine_old], axis=1),
+    )
+    old_parts = plane_gather(old)
+    wq_parts = plane_gather(chip_block(*columns(w_query, q_heads * HD, 0)))
+    mine_k, theirs_k = columns(w_key, HD, 2 * z * HD)
+    mine_v, theirs_v = columns(w_value, HD, 2 * z * HD)
+    wkv_parts = plane_gather(
+        chip_block(
+            jnp.concatenate([mine_k, mine_v], axis=1), jnp.concatenate([theirs_k, theirs_v], axis=1)
+        )
+    )
+
+    span = old.shape[1]
+    kv = jnp.zeros((2, 4 * span, HD), jnp.bfloat16)
+    for index, part in enumerate(old_parts[:3]):
+        kv = lax.dynamic_update_slice(kv, part, (0, (chip ^ index) * span, 0))
+    kv = lax.dynamic_update_slice(kv, old_parts[3], (0, (chip ^ 3) * span, 0))
+    kv = lax.dynamic_update_slice(kv, old_parts[4], (1, (chip ^ 3) * span, 0))
+
+    whole = jnp.zeros((chip_tok, depth), jnp.bfloat16)
+    for piece, place in ((stream, z),) + line_gather(stream, z):
+        whole = lax.dynamic_update_slice(whole, piece, (core * tok, place * feat))
+        whole = lax.dynamic_update_slice(whole, swap(piece, 1), ((1 - core) * tok, place * feat))
+
+    gain = norm_gain[None, :]
+    scale = math.log2(math.e) / math.sqrt(HD)
+    q = project(where, whole, gain, wq_parts, cosine, sinus, q_heads, q_heads, scale)
+    m, acc = attend_prefix(bounds, q, n_wide, kv)
+    kv_new = project(where, whole, gain, wkv_parts, cosine, sinus, 2, 1, 1.0)
+    before = lax.ppermute(kv_new[:, tok:], "ctx", [(i, i + 2) for i in range(N_CTX - 2)])
+    k_near = jnp.concatenate([before[0], kv_new[0]], axis=0)
+    v_near = jnp.concatenate([before[1], kv_new[1]], axis=0)
+    attended = attend_new(q, lo_wide, k_near, v_near, m, acc)
+
+    rows = w_out.shape[0] // 4
+    moved = [
+        lax.ppermute(
+            w_out[j * rows : (j + 1) * rows],
+            ("ctx", "tp"),
+            [
+                ((2 * k + s) * N_TP + t, (2 * (t ^ j) + s) * N_TP + k)
+                for k in range(4)
+                for s in range(2)
+                for t in range(4)
+            ],
+        )
+        for j in range(4)
+    ]
+    wo_parts = plane_gather(jnp.concatenate(moved, axis=0))
+
+    width = attended.shape[1]
+    heads_all = jnp.zeros((chip_tok, 2 * width * N_TP), jnp.bfloat16)
+    for piece, place in ((attended, z),) + line_gather(attended, z):
+        base = place * 2 * width
+        heads_all = lax.dynamic_update_slice(heads_all, piece, (0, base + core * width))
+        heads_all = lax.dynamic_update_slice(
+            heads_all, swap(piece, 1), (0, base + (1 - core) * width)
+        )
+    projected = out_project(where, heads_all, wo_parts)
+    mine = lax.dynamic_slice_in_dim(projected, core * tok, tok, 0)
+    theirs = swap(lax.dynamic_slice_in_dim(projected, (1 - core) * tok, tok, 0), 1)
+    head_share = jnp.where(
+        first,
+        jnp.concatenate([mine, theirs], axis=1),
+        jnp.concatenate([theirs, mine], axis=1),
+    ).astype(jnp.float32)
+
+    pending_share = lax.psum_scatter(
+        pending[0], "tp", scatter_dimension=1, tiled=True
+    ).astype(jnp.float32)
+    return (stream.astype(jnp.float32) + (head_share + pending_share)).astype(jnp.bfloat16)
 
 
 def solution(mesh):
@@ -190,6 +654,11 @@
         P(),
     )
     out_specs = P("ctx", "tp")
+    small = mesh.shape["ctx"] == N_CTX and mesh.shape["tp"] == N_TP
     return jax.shard_map(
-        per_device, mesh=mesh, in_specs=in_specs, out_specs=out_specs, check_vma=False
-    )
+        per_device if small else per_device_any,
+        mesh=mesh,
+        in_specs=in_specs,
+        out_specs=out_specs,
+        check_vma=False,
+    )

time: 685 us -> 600 us (0.88); the launches traced: 684 us -> 592 us
  waiting for transfers between devices: 439 us -> 172 us
  starting transfers between devices: 0.28 us -> 151 us
  matrix products: 140 us -> 0 us
  local copies, waits for them, and re-layouts: 7.01 us -> 131 us
  Pallas kernels: 0 us -> 81.3 us
  other arithmetic: 74.9 us -> 42.9 us
  blocking collectives: 9.23 us -> 0 us
    all_gather x6 -> x0, waiting for transfers between devices: 276 us -> none  [the longest x1 113 us: per_device(): whole = lax.all_gather(stream, 'tp', axis=1, tiled=True).astype(jnp.float32)]
    ppermute x0 -> x49, waiting for transfers between devices: none -> 172 us  [the longest x6 116 us: down(): lax.ppermute(v, 'tp', [(N_TP - 1 - i, N_TP - 2 - i) for i in range(first,...]
    reduce_scatter x2 -> x1, waiting for transfers between devices: 161 us -> 0.01 us  [per_device(): lax.psum_scatter(pending[0], 'tp', scatter_dimension=1, tiled=True)]
    ppermute x0 -> x49, starting transfers between devices: none -> 151 us  [the longest x4 61.7 us: per_device(): lax.ppermute(w_out[j * rows:(j + 1) * rows], ('ctx', 'tp'), [((2 * k + s)...]
    dot_general x6 -> x0, matrix products: 140 us -> none  [the longest x1 52.1 us: update(): jnp.einsum('hrd,hnd->hrn', grouped, key_block, preferred_element_type=jnp...]
    dynamic_update_slice x0 -> x14, local copies, waits for them, and re-layouts: none -> 89.8 us  [the longest x4 60 us: per_device(): lax.dynamic_update_slice(whole, swap(piece, 1), ((1 - core) * tok, place...]
    pallas_call x0 -> x5, Pallas kernels: none -> 81.3 us  [the longest x2 40.4 us: project(): pl.pallas_call(functools.partial(project_kernel, steps, heads, rot_heads,...]
    reduce_sum x2 -> x3, other arithmetic: 46.8 us -> 0.32 us  [the longest x1 0.12 us: per_device(): jnp.sum((prefix_segments[:, None] <= labels).astype(jnp.int32), axis=0)]
  transfers between devices with their start and end apart: 8 -> 50, of which waited for: 7 -> 14; matrix products, arithmetic and copies ran while one was open for 32% -> 28% of each run, Pallas kernels for 0% -> 14%
where the time goes in v1:
time: 600 us; the launch traced here: 592 us
  waiting for transfers between devices  172 us (29%)
  starting transfers between devices  151 us (25%)
  local copies, waits for them, and re-layouts  131 us (22%)
  Pallas kernels  81.3 us (14%)
  other arithmetic  42.9 us (7%)
  between operations  14.6 us (2%)
    ppermute x6, waiting for transfers between devices, down(): lax.ppermute(v, 'tp', [(N_TP - 1 - i, N_TP - 2 - i) for i in range(first,...  116 us
    ppermute x4, starting transfers between devices, per_device(): lax.ppermute(w_out[j * rows:(j + 1) * rows], ('ctx', 'tp'), [((2 * k + s)...  61.7 us
    dynamic_update_slice x4, local copies, waits for them, and re-layouts, per_device(): lax.dynamic_update_slice(whole, swap(piece, 1), ((1 - core) * tok, place...  60 us
    ppermute x32, waiting for transfers between devices, swap(): return lax.ppermute(x, 'ctx', [(c, c ^ bit) for c in range(N_CTX)])  53.3 us
    ppermute x32, starting transfers between devices, swap(): return lax.ppermute(x, 'ctx', [(c, c ^ bit) for c in range(N_CTX)])  51.3 us
    pallas_call x2, Pallas kernels, project(): pl.pallas_call(functools.partial(project_kernel, steps, heads, rot_heads,...  40.4 us
    ppermute x6, starting transfers between devices, up(): return lax.ppermute(v, 'tp', [(i, i + 1) for i in range(first, N_TP - 1)])  26.4 us
    pallas_call x1, Pallas kernels, out_project(): pl.pallas_call(functools.partial(out_kernel, steps), out_shape=jax.ShapeD...  18.1 us
  transfers between devices with their start and end apart: 50, of which 14 were waited for; matrix products, arithmetic and copies ran while one was open for 28% of the time, Pallas kernels for 14%

profile of v1, /device:TPU:0, one launch (start us, length us, event | category | flops | bytes accessed | tf_op | source)
XLA Modules:
  0.0 592.3 jit_solution(10970698544690026544)
XLA Ops:
  8.3 6.3 %collective-permute-start.2 = (bf16[384,2048]{1,0:T(8,128)(2,1)}, bf16[384,2048]{1,0:T(8,128)(2,1)}, u32[]{:S(2)}, u32[]{:S(2)}) collective-permute-start(bf16[384,2048]{1,0:T(8,128)(2,1)} %param.12), channel_id=1, source_target_pairs={{0,1},{1,2},{2,3},{4,5},{5,6},{6,7},{8,9},{9,10},{10,11},{12,13},{... | collective-permute-start | bytes 4718600 | tf_op jit(solution)/shard_map/ppermute | solution.py:180
  16.9 6.1 %broadcast_in_dim.13 = bf16[768,8192]{1,0:T(8,128)(2,1)} broadcast(bf16[]{:T(256)} %constant.85.clone.1), dimensions={} | broadcast | bytes 12582914 | tf_op jit(solution)/shard_map/broadcast_in_dim | solution.py:587
  23.0 15.6 %dynamic_update_slice.63 = bf16[768,8192]{1,0:T(8,128)(2,1)} dynamic-update-slice(bf16[768,8192]{1,0:T(8,128)(2,1)} %broadcast_in_dim.13, bf16[384,2048]{1,0:T(8,128)(2,1)S(1)} %copy-done, s32[]{:T(128)S(6)} %select_n.222, s32[]{:T(128)S(6)} %select_n.223) | dynamic-update-slice | bytes 3145732 | tf_op jit(solution)/shard_map/dynamic_update_slice | solution.py:589
  38.6 15.4 %dynamic_update_slice.64 = bf16[768,8192]{1,0:T(8,128)(2,1)} dynamic-update-slice(bf16[768,8192]{1,0:T(8,128)(2,1)} %dynamic_update_slice.63, bf16[384,2048]{1,0:T(8,128)(2,1)} %collective-permute-done, s32[]{:T(128)S(6)} %select_n.224, s32[]{:T(128)S(6)} %select_n.223) | dynamic-update-slice | bytes 3145732 | tf_op jit(solution)/shard_map/dynamic_update_slice | solution.py:590
  77.4 15.4 %dynamic_update_slice.66 = bf16[768,8192]{1,0:T(8,128)(2,1)} dynamic-update-slice(bf16[768,8192]{1,0:T(8,128)(2,1)} %get-tuple-element.25, bf16[384,2048]{1,0:T(8,128)(2,1)} %collective-permute-done.3, s32[]{:T(128)S(6)} %select_n.224, s32[]{:T(128)S(6)} %select_n.228) | dynamic-update-slice | bytes 3145732 | tf_op jit(solution)/shard_map/dynamic_update_slice | solution.py:590
  92.7 59.1 %collective-permute-done.4 = bf16[384,2048]{1,0:T(8,128)(2,1)} collective-permute-done((bf16[384,2048]{1,0:T(8,128)(2,1)S(1)}, bf16[384,2048]{1,0:T(8,128)(2,1)}, u32[]{:S(2)}, u32[]{:S(2)}) %collective-permute-start.4) | collective-permute-done | bytes 1572896 | tf_op jit(solution)/shard_map/ppermute | solution.py:183
  178.2 15.4 %dynamic_update_slice.68 = bf16[768,8192]{1,0:T(8,128)(2,1)} dynamic-update-slice(bf16[768,8192]{1,0:T(8,128)(2,1)} %get-tuple-element.23, bf16[384,2048]{1,0:T(8,128)(2,1)} %collective-permute-done.6, s32[]{:T(128)S(6)} %select_n.224, s32[]{:T(128)S(6)} %select_n.231) | dynamic-update-slice | bytes 3145732 | tf_op jit(solution)/shard_map/dynamic_update_slice | solution.py:590
  193.6 36.6 %collective-permute-done.7 = bf16[384,2048]{1,0:T(8,128)(2,1)} collective-permute-done((bf16[384,2048]{1,0:T(8,128)(2,1)}, bf16[384,2048]{1,0:T(8,128)(2,1)}, u32[]{:S(2)}, u32[]{:S(2)}) %collective-permute-start.7) | collective-permute-done | bytes 1572896 | tf_op jit(solution)/shard_map/ppermute | solution.py:183
  233.4 5.1 fusion.6
  247.4 9.2 %collective-permute-done.20.rest_1_ = bf16[2048,256]{1,0:T(8,128)(2,1)} collective-permute-done((bf16[2048,256]{1,0:T(8,128)(2,1)}, bf16[2048,256]{1,0:T(8,128)(2,1)}, u32[]{:S(2)}, u32[]{:S(2)}) %collective-permute-start.20) | collective-permute-done | bytes 1048608 | tf_op jit(solution)/shard_map/ppermute | solution.py:175
  277.0 13.8 %dynamic_update_slice.70.x_ref = bf16[768,8192]{1,0:T(8,128)(2,1)} dynamic-update-slice(bf16[768,8192]{1,0:T(8,128)(2,1)} %get-tuple-element.21, bf16[384,2048]{1,0:T(8,128)(2,1)S(1)} %collective-permute-done.9, s32[]{:T(128)S(6)} %select_n.224, s32[]{:T(128)S(6)} %select_n.240) | dynamic-update-slice | bytes 3145732 | tf_op jit(solution)/shard_map/dynamic_update_slice | solution.py:590
  290.8 21.5 %collective-permute-done.22.rest_3_ = bf16[1024,256]{1,0:T(8,128)(2,1)S(1)} collective-permute-done((bf16[1024,256]{1,0:T(8,128)(2,1)S(1)}, bf16[1024,256]{1,0:T(8,128)(2,1)S(1)}, u32[]{:S(2)}, u32[]{:S(2)}) %collective-permute-start.22) | collective-permute-done | bytes 524320 | tf_op jit(solution)/shard_map/ppermute | solution.py:175
  313.8 15.3 %collective-permute-start.42 = (bf16[256,1024]{1,0:T(8,128)(2,1)}, bf16[256,1024]{1,0:T(8,128)(2,1)}, u32[]{:S(2)}, u32[]{:S(2)}) collective-permute-start(bf16[256,1024]{1,0:T(8,128)(2,1)} %get-tuple-element.32), channel_id=1, source_target_pairs={{0,16},{1,24},{2,0},{3,8},{4,20},{5,28},{6,4},{7,12},{8,17},{9,25}... | collective-permute-start | bytes 1572872 | tf_op jit(solution)/shard_map/ppermute | solution.py:604
  329.2 18.6 %shard_map.119 = bf16[2,768,128]{2,1,0:T(8,128)(2,1)} custom-call(s32[2]{0:T(128)} %pad_add_fusion.3.where_ref, bf16[768,8192]{1,0:T(8,128)(2,1)} %dynamic_update_slice.70.x_ref, bf16[1,8192]{1,0:T(2,128)(2,1)} %broadcast_in_dim.14.gain_ref, bf16[2048,256]{1,0:T(8,128)(2,1)} %pad_maximum_fusion.1.rest_0_, bf16[2048,256]{1,0:T(8,128)(2,1)} %collective-permute-done.20.rest_1_, ...), custom_call_target="tpu_custom_call" | custom-call | flops 3221225472 | bytes 16777216 | tf_op jit(solution)/shard_map/pallas_call | solution.py:281
  352.2 21.8 %shard_map.118.q_ref = bf16[4,768,128]{2,1,0:T(8,128)(2,1)} custom-call(s32[2]{0:T(128)} %pad_add_fusion.3.where_ref, bf16[768,8192]{1,0:T(8,128)(2,1)} %dynamic_update_slice.70.x_ref, bf16[1,8192]{1,0:T(2,128)(2,1)} %broadcast_in_dim.14.gain_ref, bf16[2048,512]{1,0:T(8,128)(2,1)} %pad_maximum_fusion.rest_0_, ...), custom_call_target="tpu_custom_call" | custom-call | flops 6442450944 | bytes 20971520 | tf_op jit(solution)/shard_map/pallas_call | solution.py:281
  374.9 15.9 %shard_map.120 = (f32[3,2,512,128]{3,2,1,0:T(8,128)}, f32[3,2,512,256]{3,2,1,0:T(8,128)}) custom-call(s32[2,3]{1,0:T(2,128)} %pad_add_fusion.2.bound_ref, bf16[4,768,128]{2,1,0:T(8,128)(2,1)} %shard_map.118.q_ref, s32[768,128]{1,0:T(8,128)} %broadcast_in_dim.16.n_ref, bf16[2,6144,128]{2,1,0:T(8,128)(2,1)} %constant_dynamic-update-slice_fusion.12.kv_ref), custom_call_target="tpu_custom_call" | custom-call | flops 19327352832 | bytes 3145728 | tf_op jit(solution)/shard_map/pallas_call | solution.py:365
  393.3 6.8 %shard_map.121 = bf16[768,512]{1,0:T(8,128)(2,1)} custom-call(bf16[4,768,128]{2,1,0:T(8,128)(2,1)} %shard_map.118.q_ref, s32[768,128]{1,0:T(8,128)} %broadcast_in_dim.15.lo_ref, bf16[1152,128]{1,0:T(8,128)(2,1)} %pad_maximum_fusion.5.k_ref, bf16[1152,128]{1,0:T(8,128)(2,1)} %pad_maximum_fusion.6.v_ref, f32[3,2,512,128]{3,2,1,0:T(8,128)} %get-tuple-element.7.m_ref, ...), custom_call_target="tpu_custom_call" | custom-call | flops 2013265920 | bytes 6291456 | tf_op jit(solution)/shard_map/pallas_call | solution.py:429
  400.1 44.2 %collective-permute-start.43 = (bf16[256,1024]{1,0:T(8,128)(2,1)}, bf16[256,1024]{1,0:T(8,128)(2,1)}, u32[]{:S(2)}, u32[]{:S(2)}) collective-permute-start(bf16[256,1024]{1,0:T(8,128)(2,1)} %get-tuple-element.29), channel_id=1, source_target_pairs={{0,24},{1,16},{2,8},{3,0},{4,28},{5,20},{6,12},{7,4},{8,25},{9,17}... | collective-permute-start | bytes 1572872 | tf_op jit(solution)/shard_map/ppermute | solution.py:604
  445.6 13.3 %collective-permute-start.32 = (bf16[768,512]{1,0:T(8,128)(2,1)}, bf16[768,512]{1,0:T(8,128)(2,1)S(1)}, u32[]{:S(2)}, u32[]{:S(2)}) collective-permute-start(bf16[768,512]{1,0:T(8,128)(2,1)} %shard_map.121), channel_id=1, source_target_pairs={{0,1},{1,2},{2,3},{4,5},{5,6},{6,7},{8,9},{9,10},{10,11},{12,13},{... | collective-permute-start | bytes 2359304 | tf_op jit(solution)/shard_map/ppermute | solution.py:180
  469.5 15.1 %collective-permute-start.45 = (bf16[1024,1024]{1,0:T(8,128)(2,1)}, bf16[1024,1024]{1,0:T(8,128)(2,1)}, u32[]{:S(2)}, u32[]{:S(2)}) collective-permute-start(bf16[1024,1024]{1,0:T(8,128)(2,1)} %constant_dynamic-update-slice_fusion.rest_0_), channel_id=1, source_target_pairs={{0,16},{4,20},{8,24},{12,28},{16,0},{20,4},{24,8},{28,12},{1,17},{... | collective-permute-start | bytes 6291464 | tf_op jit(solution)/shard_map/ppermute | solution.py:175
  497.8 16.9 %collective-permute-done.34 = bf16[768,512]{1,0:T(8,128)(2,1)} collective-permute-done((bf16[768,512]{1,0:T(8,128)(2,1)S(1)}, bf16[768,512]{1,0:T(8,128)(2,1)}, u32[]{:S(2)}, u32[]{:S(2)}) %collective-permute-start.34) | collective-permute-done | bytes 786464 | tf_op jit(solution)/shard_map/ppermute | solution.py:183
  522.3 11.7 %collective-permute-start.46 = (bf16[512,1024]{1,0:T(8,128)(2,1)}, bf16[512,1024]{1,0:T(8,128)(2,1)}, u32[]{:S(2)}, u32[]{:S(2)}) collective-permute-start(bf16[512,1024]{1,0:T(8,128)(2,1)} %slice.97), channel_id=1, source_target_pairs={{0,16},{4,20},{8,24},{12,28},{16,0},{20,4},{24,8},{28,12},{1,17},{... | collective-permute-start | bytes 3145736 | tf_op jit(solution)/shard_map/ppermute | solution.py:175
  548.5 7.5 %collective-permute-done.46.rest_3_ = bf16[512,1024]{1,0:T(8,128)(2,1)} collective-permute-done((bf16[512,1024]{1,0:T(8,128)(2,1)}, bf16[512,1024]{1,0:T(8,128)(2,1)}, u32[]{:S(2)}, u32[]{:S(2)}) %collective-permute-start.46) | collective-permute-done | bytes 1048608 | tf_op jit(solution)/shard_map/ppermute | solution.py:175
  559.7 18.1 %shard_map.122 = bf16[768,1024]{1,0:T(8,128)(2,1)} custom-call(s32[2]{0:T(128)} %pad_add_fusion.3.where_ref, bf16[768,4096]{1,0:T(8,128)(2,1)} %constant_dynamic-update-slice_fusion.4.x_ref, bf16[1024,1024]{1,0:T(8,128)(2,1)} %constant_dynamic-update-slice_fusion.rest_0_, bf16[1024,1024]{1,0:T(8,128)(2,1)} %collective-permute-done.44.rest_1_, ...), custom_call_target="tpu_custom_call" | custom-call | flops 6442450944 | bytes 14680064 | tf_op jit(solution)/shard_map/pallas_call | solution.py:479
  (192 shorter events, 153.0 us)
Async XLA Ops:
  6.5 575.1 %reduce-scatter.2.cloned.1.call-start = ((), (), s32[]{:S(2)}) async-start(), calls=%async_computation.1 | async-start | bytes 7864320 | tf_op jit(solution)/shard_map/reduce_scatter | solution.py:635
  7.0 47.0 %collective-permute-start.1 = (bf16[384,2048]{1,0:T(8,128)(2,1)}, bf16[384,2048]{1,0:T(8,128)(2,1)S(1)}, u32[]{:S(2)}, u32[]{:S(2)}) collective-permute-start(bf16[384,2048]{1,0:T(8,128)(2,1)} %param.12), channel_id=1, source_target_pairs={{3,2},{2,1},{1,0},{7,6},{6,5},{5,4},{11,10},{10,9},{9,8},{15,14},{... | collective-permute-start | bytes 4718600 | tf_op jit(solution)/shard_map/ppermute | solution.py:183
  8.3 45.8 %collective-permute-start.2 = (bf16[384,2048]{1,0:T(8,128)(2,1)}, bf16[384,2048]{1,0:T(8,128)(2,1)}, u32[]{:S(2)}, u32[]{:S(2)}) collective-permute-start(bf16[384,2048]{1,0:T(8,128)(2,1)} %param.12), channel_id=1, source_target_pairs={{0,1},{1,2},{2,3},{4,5},{5,6},{6,7},{8,9},{9,10},{10,11},{12,13},{... | collective-permute-start | bytes 4718600 | tf_op jit(solution)/shard_map/ppermute | solution.py:180
  16.7 55.6 %collective-permute-start.25 = (bf16[2,768,128]{2,1,0:T(8,128)(2,1)}, bf16[2,768,128]{2,1,0:T(8,128)(2,1)}, u32[]{:S(2)}, u32[]{:S(2)}) collective-permute-start(bf16[2,768,128]{2,1,0:T(8,128)(2,1)} %get-tuple-element.27), channel_id=1, source_target_pairs={{0,4},{4,0},{8,12},{12,8},{16,20},{20,16},{24,28},{28,24},{1,5},{5... | collective-permute-start | bytes 1179656 | tf_op jit(solution)/shard_map/ppermute | solution.py:175
  56.8 95.0 %collective-permute-start.4 = (bf16[384,2048]{1,0:T(8,128)(2,1)S(1)}, bf16[384,2048]{1,0:T(8,128)(2,1)}, u32[]{:S(2)}, u32[]{:S(2)}) collective-permute-start(bf16[384,2048]{1,0:T(8,128)(2,1)S(1)} %collective-permute-done.1), channel_id=1, source_target_pairs={{2,1},{1,0},{6,5},{5,4},{10,9},{9,8},{14,13},{13,12},{18,17},{17,1... | collective-permute-start | bytes 4718600 | tf_op jit(solution)/shard_map/ppermute | solution.py:183
  58.1 96.0 %collective-permute-start.5 = (bf16[384,2048]{1,0:T(8,128)(2,1)}, bf16[384,2048]{1,0:T(8,128)(2,1)}, u32[]{:S(2)}, u32[]{:S(2)}) collective-permute-start(bf16[384,2048]{1,0:T(8,128)(2,1)} %collective-permute-done.2), channel_id=1, source_target_pairs={{1,2},{2,3},{5,6},{6,7},{9,10},{10,11},{13,14},{14,15},{17,18},{18... | collective-permute-start | bytes 4718600 | tf_op jit(solution)/shard_map/ppermute | solution.py:180
  71.5 88.3 %collective-permute-start.10 = (bf16[1024,512]{1,0:T(8,128)(2,1)}, bf16[1024,512]{1,0:T(8,128)(2,1)S(1)}, u32[]{:S(2)}, u32[]{:S(2)}) collective-permute-start(bf16[1024,512]{1,0:T(8,128)(2,1)} %get-tuple-element.38), channel_id=1, source_target_pairs={{0,4},{4,0},{8,12},{12,8},{16,20},{20,16},{24,28},{28,24},{1,5},{5... | collective-permute-start | bytes 3145736 | tf_op jit(solution)/shard_map/ppermute | solution.py:175
  72.2 86.3 %collective-permute-start.15 = (s32[384]{0:T(512)S(1)}, s32[384]{0:T(512)S(1)}, u32[]{:S(2)}, u32[]{:S(2)}) collective-permute-start(s32[384]{0:T(512)S(1)} %copy-done.15), channel_id=1, source_target_pairs={{0,4},{4,0},{8,12},{12,8},{16,20},{20,16},{24,28},{28,24},{1,5},{5... | collective-permute-start | bytes 4616 | tf_op jit(solution)/shard_map/ppermute | solution.py:175
  75.5 82.4 %collective-permute-start.18 = (s32[2,16]{1,0:T(2,128)S(1)}, s32[2,16]{1,0:T(2,128)S(1)}, u32[]{:S(2)}, u32[]{:S(2)}) collective-permute-start(s32[2,16]{1,0:T(2,128)S(1)} %fusion.10), channel_id=1, source_target_pairs={{0,16},{4,20},{8,24},{12,28},{16,0},{20,4},{24,8},{28,12},{1,17},{... | collective-permute-start | bytes 392 | tf_op jit(solution)/shard_map/ppermute | solution.py:175
  158.5 71.6 %collective-permute-start.7 = (bf16[384,2048]{1,0:T(8,128)(2,1)}, bf16[384,2048]{1,0:T(8,128)(2,1)}, u32[]{:S(2)}, u32[]{:S(2)}) collective-permute-start(bf16[384,2048]{1,0:T(8,128)(2,1)} %collective-permute-done.4), channel_id=1, source_target_pairs={{1,0},{5,4},{9,8},{13,12},{17,16},{21,20},{25,24},{29,28}} | collective-permute-start | bytes 4718600 | tf_op jit(solution)/shard_map/ppermute | solution.py:183
  160.8 71.1 %collective-permute-start.8 = (bf16[384,2048]{1,0:T(8,128)(2,1)}, bf16[384,2048]{1,0:T(8,128)(2,1)}, u32[]{:S(2)}, u32[]{:S(2)}) collective-permute-start(bf16[384,2048]{1,0:T(8,128)(2,1)} %collective-permute-done.5), channel_id=1, source_target_pairs={{2,3},{6,7},{10,11},{14,15},{18,19},{22,23},{26,27},{30,31}} | collective-permute-start | bytes 4718600 | tf_op jit(solution)/shard_map/ppermute | solution.py:180
  172.4 68.3 %collective-permute-start.11 = (bf16[2048,512]{1,0:T(8,128)(2,1)}, bf16[2048,512]{1,0:T(8,128)(2,1)}, u32[]{:S(2)}, u32[]{:S(2)}) collective-permute-start(bf16[2048,512]{1,0:T(8,128)(2,1)} %pad_maximum_fusion.rest_0_), channel_id=1, source_target_pairs={{0,8},{4,12},{8,0},{12,4},{16,24},{20,28},{24,16},{28,20},{1,9},{5... | collective-permute-start | bytes 6291464 | tf_op jit(solution)/shard_map/ppermute | solution.py:175
  172.5 70.0 %collective-permute-start.12 = (bf16[2048,512]{1,0:T(8,128)(2,1)}, bf16[2048,512]{1,0:T(8,128)(2,1)}, u32[]{:S(2)}, u32[]{:S(2)}) collective-permute-start(bf16[2048,512]{1,0:T(8,128)(2,1)} %pad_maximum_fusion.rest_0_), channel_id=1, source_target_pairs={{0,16},{4,20},{8,24},{12,28},{16,0},{20,4},{24,8},{28,12},{1,17},{... | collective-permute-start | bytes 6291464 | tf_op jit(solution)/shard_map/ppermute | solution.py:175
  176.0 62.5 %collective-permute-start.27 = (bf16[2,1536,128]{2,1,0:T(8,128)(2,1)}, bf16[2,1536,128]{2,1,0:T(8,128)(2,1)}, u32[]{:S(2)}, u32[]{:S(2)}) collective-permute-start(bf16[2,1536,128]{2,1,0:T(8,128)(2,1)} %get-tuple-element.20), channel_id=1, source_target_pairs={{0,16},{4,20},{8,24},{12,28},{16,0},{20,4},{24,8},{28,12},{1,17},{... | collective-permute-start | bytes 2359304 | tf_op jit(solution)/shard_map/ppermute | solution.py:175
  256.5 92.2 %collective-permute-start.13 = (bf16[1024,512]{1,0:T(8,128)(2,1)S(1)}, bf16[1024,512]{1,0:T(8,128)(2,1)}, u32[]{:S(2)}, u32[]{:S(2)}) collective-permute-start(bf16[1024,512]{1,0:T(8,128)(2,1)S(1)} %slice.84), channel_id=1, source_target_pairs={{0,16},{4,20},{8,24},{12,28},{16,0},{20,4},{24,8},{28,12},{1,17},{... | collective-permute-start | bytes 3145736 | tf_op jit(solution)/shard_map/ppermute | solution.py:175
  260.7 91.5 %collective-permute-start.14 = (bf16[1024,512]{1,0:T(8,128)(2,1)S(1)}, bf16[1024,512]{1,0:T(8,128)(2,1)}, u32[]{:S(2)}, u32[]{:S(2)}) collective-permute-start(bf16[1024,512]{1,0:T(8,128)(2,1)S(1)} %slice.85), channel_id=1, source_target_pairs={{0,8},{4,12},{8,0},{12,4},{16,24},{20,28},{24,16},{28,20},{1,9},{5... | collective-permute-start | bytes 3145736 | tf_op jit(solution)/shard_map/ppermute | solution.py:175
  276.3 168.0 %collective-permute-start.40 = (bf16[256,1024]{1,0:T(8,128)(2,1)S(1)}, bf16[256,1024]{1,0:T(8,128)(2,1)S(1)}, u32[]{:S(2)}, u32[]{:S(2)}) collective-permute-start(bf16[256,1024]{1,0:T(8,128)(2,1)S(1)} %copy-done.12), channel_id=1, source_target_pairs={{0,0},{1,8},{2,16},{3,24},{4,4},{5,12},{6,20},{7,28},{8,1},{9,9},{... | collective-permute-start | bytes 1572872 | tf_op jit(solution)/shard_map/ppermute | solution.py:604
  312.3 133.3 %collective-permute-start.41 = (bf16[256,1024]{1,0:T(8,128)(2,1)S(1)}, bf16[256,1024]{1,0:T(8,128)(2,1)}, u32[]{:S(2)}, u32[]{:S(2)}) collective-permute-start(bf16[256,1024]{1,0:T(8,128)(2,1)S(1)} %copy-done.11), channel_id=1, source_target_pairs={{0,8},{1,0},{2,24},{3,16},{4,12},{5,4},{6,28},{7,20},{8,9},{9,1},{... | collective-permute-start | bytes 1572872 | tf_op jit(solution)/shard_map/ppermute | solution.py:604
  313.8 148.9 %collective-permute-start.42 = (bf16[256,1024]{1,0:T(8,128)(2,1)}, bf16[256,1024]{1,0:T(8,128)(2,1)}, u32[]{:S(2)}, u32[]{:S(2)}) collective-permute-start(bf16[256,1024]{1,0:T(8,128)(2,1)} %get-tuple-element.32), channel_id=1, source_target_pairs={{0,16},{1,24},{2,0},{3,8},{4,20},{5,28},{6,4},{7,12},{8,17},{9,25}... | collective-permute-start | bytes 1572872 | tf_op jit(solution)/shard_map/ppermute | solution.py:604
  400.1 89.0 %collective-permute-start.30 = (bf16[768,512]{1,0:T(8,128)(2,1)}, bf16[768,512]{1,0:T(8,128)(2,1)}, u32[]{:S(2)}, u32[]{:S(2)}) collective-permute-start(bf16[768,512]{1,0:T(8,128)(2,1)} %shard_map.121), channel_id=1, source_target_pairs={{0,4},{4,0},{8,12},{12,8},{16,20},{20,16},{24,28},{28,24},{1,5},{5... | collective-permute-start | bytes 2359304 | tf_op jit(solution)/shard_map/ppermute | solution.py:175
  400.1 67.5 %collective-permute-start.43 = (bf16[256,1024]{1,0:T(8,128)(2,1)}, bf16[256,1024]{1,0:T(8,128)(2,1)}, u32[]{:S(2)}, u32[]{:S(2)}) collective-permute-start(bf16[256,1024]{1,0:T(8,128)(2,1)} %get-tuple-element.29), channel_id=1, source_target_pairs={{0,24},{1,16},{2,8},{3,0},{4,28},{5,20},{6,12},{7,4},{8,25},{9,17}... | collective-permute-start | bytes 1572872 | tf_op jit(solution)/shard_map/ppermute | solution.py:604
  444.3 47.0 %collective-permute-start.31 = (bf16[768,512]{1,0:T(8,128)(2,1)}, bf16[768,512]{1,0:T(8,128)(2,1)S(1)}, u32[]{:S(2)}, u32[]{:S(2)}) collective-permute-start(bf16[768,512]{1,0:T(8,128)(2,1)} %shard_map.121), channel_id=1, source_target_pairs={{3,2},{2,1},{1,0},{7,6},{6,5},{5,4},{11,10},{10,9},{9,8},{15,14},{... | collective-permute-start | bytes 2359304 | tf_op jit(solution)/shard_map/ppermute | solution.py:183
  469.5 50.5 %collective-permute-start.44 = (bf16[1024,1024]{1,0:T(8,128)(2,1)}, bf16[1024,1024]{1,0:T(8,128)(2,1)}, u32[]{:S(2)}, u32[]{:S(2)}) collective-permute-start(bf16[1024,1024]{1,0:T(8,128)(2,1)} %constant_dynamic-update-slice_fusion.rest_0_), channel_id=1, source_target_pairs={{0,8},{4,12},{8,0},{12,4},{16,24},{20,28},{24,16},{28,20},{1,9},{5... | collective-permute-start | bytes 6291464 | tf_op jit(solution)/shard_map/ppermute | solution.py:175
  469.5 64.5 %collective-permute-start.45 = (bf16[1024,1024]{1,0:T(8,128)(2,1)}, bf16[1024,1024]{1,0:T(8,128)(2,1)}, u32[]{:S(2)}, u32[]{:S(2)}) collective-permute-start(bf16[1024,1024]{1,0:T(8,128)(2,1)} %constant_dynamic-update-slice_fusion.rest_0_), channel_id=1, source_target_pairs={{0,16},{4,20},{8,24},{12,28},{16,0},{20,4},{24,8},{28,12},{1,17},{... | collective-permute-start | bytes 6291464 | tf_op jit(solution)/shard_map/ppermute | solution.py:175
  (45 other events, 848.3 us)
Sparse Core Ops, SparseCore 0:
  61.2 153.0 reduce-scatter.1

commit v2 on v0

--- a/solution.py
+++ b/solution.py
@@ -1,13 +1,17 @@
+import functools
 import math
 
 import jax
 import jax.numpy as jnp
 from jax import lax
+from jax.experimental import pallas as pl
+from jax.experimental.pallas import tpu as pltpu
 from jax.sharding import PartitionSpec as P
 
 HQ = 32
 KVH = 8
 HD = 128
+NTRAJ = 16
 
 
 ROPE_BASE = 500000.0
@@ -51,13 +55,12 @@
     return jnp.where(is_prefix[None, :], earlier, same)
 
 
-def update(carry, grouped, key_block, value_block, seen):
-    running_max, totals, numerator = carry
+def attend_whole(grouped, key_block, value_block, seen):
     scores = jnp.einsum("hrd,hnd->hrn", grouped, key_block, preferred_element_type=jnp.float32) * (
         1.0 / math.sqrt(HD)
     )
     scores = jnp.where(seen[None], scores, MASKED)
-    new_max = jnp.maximum(running_max, jnp.max(scores, axis=2))
+    new_max = jnp.max(scores, axis=2)
     weights = jnp.where(seen[None], jnp.exp(scores - new_max[..., None]), 0.0)
     totals = jnp.sum(weights, axis=2)
     numerator = jnp.einsum(
@@ -66,18 +69,10 @@
         value_block,
         preferred_element_type=jnp.float32,
     )
-    return (new_max, totals, numerator)
-
-
-def empty_state(kv_heads, row_count):
-    return (
-        jnp.full((kv_heads, row_count), MASKED, jnp.float32),
-        jnp.zeros((kv_heads, row_count), jnp.float32),
-        jnp.zeros((kv_heads, row_count, HD), jnp.float32),
-    )
-
-
-def per_device(
+    return numerator / totals[..., None]
+
+
+def per_device_any(
     stream,
     pending,
     norm_gain,
@@ -147,10 +142,7 @@
     within = absolute % key_span
     key_pos = absolute // key_span * tok_rows + within - prefix_rows
     seen = visibility(label_block[0, 0], within < prefix_rows, key_pos, query_segs, query_index)
-    running_max, totals, numerator = update(
-        empty_state(kv_heads, tok_rows * group_size), grouped, kv_block[0], kv_block[1], seen
-    )
-    attended_heads = (numerator / totals[..., None]).astype(jnp.bfloat16)
+    attended_heads = attend_whole(grouped, kv_block[0], kv_block[1], seen).astype(jnp.bfloat16)
     attended = jnp.transpose(
         attended_heads.reshape(kv_heads, tok_rows, group_size, HD), (1, 0, 2, 3)
     ).reshape(tok_rows, q_cols)
@@ -172,6 +164,526 @@
     )
     block_share = head_share + pending_share
     return (stream.astype(jnp.float32) + block_share).astype(jnp.bfloat16)
+
+
+N_CTX = 8
+N_TP = 4
+MIB = 1024 * 1024
+
+
+def swap(x, bit):
+    return lax.ppermute(x, "ctx", [(c, c ^ bit) for c in range(N_CTX)])
+
+
+def hop_up(v, pairs):
+    return lax.ppermute(v, "tp", [(i, i + 1) for i in pairs])
+
+
+def hop_down(v, pairs):
+    return lax.ppermute(v, "tp", [(N_TP - 1 - i, N_TP - 2 - i) for i in pairs])
+
+
+def none_of(*arrays):
+    total = jnp.float32(0)
+    for a in arrays:
+        total = total + jnp.minimum(jnp.abs(a.reshape(-1)[0].astype(jnp.float32)), 0.0)
+    return total
+
+
+def after(x, zero):
+    return x + zero.astype(x.dtype)
+
+
+def gather_steps(x, z):
+    u1, d1 = hop_up(x, (0, 1, 2)), hop_down(x, (0, 1, 2))
+    u2, d2 = hop_up(u1, (1, 2)), hop_down(d1, (1, 2))
+    u3, d3 = hop_up(u2, (2,)), hop_down(d2, (2,))
+    low = z < 2
+    a = jnp.where(low, d1, u1)
+    b = jnp.where(low, d2, u2)
+    early = jnp.where(z == 1, u1, d1)
+    c = jnp.where(z == 0, d3, jnp.where(z == 3, u3, early))
+    places = jnp.stack(
+        [z, jnp.where(low, z + 1, z - 1), jnp.where(low, z + 2, z - 2), jnp.where(z % 2 == 1, 0, 3)]
+    )
+    return ((u1, d1), (u2, d2), (u3, d3)), (x, a, b, c), places
+
+
+def rotated(v, cosine, sinus):
+    return v * cosine + pltpu.roll(v, HD // 2, 1) * sinus
+
+
+def copies_of(sems, first=0):
+    count = [first]
+
+    def make(src, dst):
+        copy = pltpu.make_async_copy(src, dst, sems.at[count[0]])
+        count[0] += 1
+        return copy
+
+    return make
+
+
+def project_kernel(heads, rot_heads, scale, ids_ref, *refs):
+    xs, ws = refs[:8], refs[8:16]
+    factor_ref, cos_ref, sin_ref, out_ref, x_buf, w_buf, x_sem, w_sem = refs[16:]
+    chip, core = ids_ref[0], ids_ref[1]
+    tok, half = xs[0].shape[0], x_buf.shape[-1]
+    mine = pl.multiple_of(core * tok, 128)
+    theirs = pl.multiple_of((1 - core) * tok, 128)
+    for r in range(4):
+        part = ids_ref[2 + r] ^ chip
+        for h in range(2):
+            cols = pl.ds(pl.multiple_of((core ^ h) * half, 128), half)
+            at = 2 * r + h
+            for m in range(4):
+
+                @pl.when(part == m)
+                def _():
+                    pltpu.make_async_copy(ws[2 * m + h], w_buf.at[at], w_sem.at[at]).start()
+
+            for s, rows in ((0, mine), (1, theirs)):
+                pltpu.make_async_copy(
+                    xs[2 * r + s].at[:, cols], x_buf.at[at, pl.ds(rows, tok)], x_sem.at[2 * at + s]
+                ).start()
+    acc = None
+    for at in range(8):
+        pltpu.make_async_copy(ws[0], w_buf.at[at], w_sem.at[at]).wait()
+        for s in range(2):
+            pltpu.make_async_copy(
+                xs[0].at[:, pl.ds(0, half)], x_buf.at[at, pl.ds(0, tok)], x_sem.at[2 * at + s]
+            ).wait()
+        term = jnp.dot(x_buf[at], w_buf[at], preferred_element_type=jnp.float32)
+        acc = term if acc is None else acc + term
+    factor = factor_ref[...]
+    for h in range(heads):
+        v = acc[:, h * HD : (h + 1) * HD] * factor
+        if h < rot_heads:
+            v = rotated(v, cos_ref[...], sin_ref[...]) * scale
+        out_ref[h] = v.astype(jnp.bfloat16)
+
+
+def project(ids, xs, ws, factor, cosine, sinus, heads, rot_heads, scale):
+    tok, feat = xs[0].shape
+    cols = heads * HD
+    half = feat // 2
+    hbm = pl.BlockSpec(memory_space=pl.ANY)
+    vmem = pl.BlockSpec(memory_space=pltpu.VMEM)
+    return pl.pallas_call(
+        functools.partial(project_kernel, heads, rot_heads, scale),
+        out_shape=jax.ShapeDtypeStruct((heads, 2 * tok, HD), jnp.bfloat16),
+        in_specs=[pl.BlockSpec(memory_space=pltpu.SMEM)] + [hbm] * 16 + [vmem] * 3,
+        out_specs=vmem,
+        scratch_shapes=[
+            pltpu.VMEM((8, 2 * tok, half), jnp.bfloat16),
+            pltpu.VMEM((8, half, cols), jnp.bfloat16),
+            pltpu.SemaphoreType.DMA((16,)),
+            pltpu.SemaphoreType.DMA((8,)),
+        ],
+        compiler_params=pltpu.CompilerParams(vmem_limit_bytes=40 * MIB),
+        cost_estimate=pl.CostEstimate(
+            flops=2 * 2 * tok * 4 * feat * cols,
+            bytes_accessed=8 * feat * (2 * tok + cols),
+            transcendentals=0,
+        ),
+    )(ids, *xs, *ws, factor, cosine, sinus)
+
+
+BT = 256
+BK = 512
+UNROLL = 2
+CHAIN = 2
+
+
+def scores(q, k):
+    return lax.dot_general(q, k, (((1,), (1,)), ((), ())), preferred_element_type=jnp.float32)
+
+
+def absorb(s, v_ext, m, acc):
+    new = jnp.maximum(m, jnp.max(s, axis=1, keepdims=True))
+    p = jnp.exp2(s - new).astype(jnp.bfloat16)
+    acc = acc * jnp.exp2(m - new) + jnp.dot(p, v_ext, preferred_element_type=jnp.float32)
+    return new, acc
+
+
+def prefix_kernel(bound_ref, q_ref, n_ref, kv_ref, m_out, acc_out, v_ext, s_ref, m_ref, acc_ref):
+    b = pl.program_id(0)
+    heads, bt = q_ref.shape[0], q_ref.shape[1]
+    rows, chains = CHAIN * bt, heads // CHAIN
+    big = UNROLL * BK
+    last = kv_ref.shape[1] // big - 1
+
+    @pl.when(b == 0)
+    def _():
+        v_ext[:, :HD] = kv_ref[1]
+        v_ext[:, HD:] = jnp.ones_like(kv_ref[1])
+
+    m_ref[...] = jnp.full_like(m_ref, MASKED)
+    acc_ref[...] = jnp.zeros_like(acc_ref)
+    n_rows = jnp.concatenate([n_ref[:, :1]] * CHAIN, axis=0)
+
+    def query(g):
+        return q_ref[g * CHAIN : (g + 1) * CHAIN].reshape(rows, HD)
+
+    s_ref[...] = scores(query(0), kv_ref[0, :BK, :])
+    items = [(u, g) for u in range(UNROLL) for g in range(chains)]
+
+    def body(kb, masked):
+        start = pl.multiple_of(kb * big, big)
+        follow = pl.multiple_of(jnp.minimum(kb + 1, last) * big, big)
+        ms = [m_ref[g][:, :1] for g in range(chains)]
+        accs = [acc_ref[g] for g in range(chains)]
+        s = s_ref[...]
+        for t, (u, g) in enumerate(items):
+            if t + 1 < len(items):
+                at, who = start + items[t + 1][0] * BK, items[t + 1][1]
+            else:
+                at, who = follow, 0
+            ahead = scores(query(who), kv_ref[0, pl.ds(at, BK), :])
+            if masked:
+                col = lax.broadcasted_iota(jnp.int32, s.shape, 1) + (start + u * BK)
+                s = jnp.where(col < n_rows, s, MASKED)
+            v = v_ext[pl.ds(start + u * BK, BK), :]
+            ms[g], accs[g] = absorb(s, v, ms[g], accs[g])
+            s = ahead
+        s_ref[...] = s
+        for g in range(chains):
+            m_ref[g] = jnp.broadcast_to(ms[g], (rows, 128))
+            acc_ref[g] = accs[g]
+
+    full = bound_ref[0, b] // big
+    some = (bound_ref[1, b] + big - 1) // big
+    lax.fori_loop(0, full, lambda kb, c: (body(kb, False), c)[1], 0)
+    lax.fori_loop(full, some, lambda kb, c: (body(kb, True), c)[1], 0)
+    m_out[0] = m_ref[...]
+    acc_out[0] = acc_ref[...]
+
+
+def attend_prefix(bounds, q, n_tok, kv):
+    heads, tokens, _ = q.shape
+    blocks = tokens // BT
+    chains, rows = heads // CHAIN, CHAIN * BT
+    keys = kv.shape[1]
+    return pl.pallas_call(
+        prefix_kernel,
+        out_shape=(
+            jax.ShapeDtypeStruct((blocks, chains, rows, 128), jnp.float32),
+            jax.ShapeDtypeStruct((blocks, chains, rows, 2 * HD), jnp.float32),
+        ),
+        grid_spec=pltpu.PrefetchScalarGridSpec(
+            num_scalar_prefetch=1,
+            grid=(blocks,),
+            in_specs=[
+                pl.BlockSpec((heads, BT, HD), lambda b, *_: (0, b, 0)),
+                pl.BlockSpec((BT, 128), lambda b, *_: (b, 0)),
+                pl.BlockSpec((2, keys, HD), lambda b, *_: (0, 0, 0)),
+            ],
+            out_specs=(
+                pl.BlockSpec((1, chains, rows, 128), lambda b, *_: (b, 0, 0, 0)),
+                pl.BlockSpec((1, chains, rows, 2 * HD), lambda b, *_: (b, 0, 0, 0)),
+            ),
+            scratch_shapes=[
+                pltpu.VMEM((keys, 2 * HD), jnp.bfloat16),
+                pltpu.VMEM((rows, BK), jnp.float32),
+                pltpu.VMEM((chains, rows, 128), jnp.float32),
+                pltpu.VMEM((chains, rows, 2 * HD), jnp.float32),
+            ],
+        ),
+        compiler_params=pltpu.CompilerParams(vmem_limit_bytes=40 * MIB),
+        cost_estimate=pl.CostEstimate(
+            flops=8 * heads * tokens * keys * HD,
+            bytes_accessed=4 * keys * HD,
+            transcendentals=heads * tokens * keys,
+        ),
+    )(bounds, q, n_tok, kv)
+
+
+def new_kernel(halo, q_ref, lo_ref, k_ref, v_ref, m_ref, acc_ref, out_ref):
+    b = pl.program_id(0)
+    heads, bt = q_ref.shape[0], q_ref.shape[1]
+    rows = CHAIN * bt
+    span = halo + bt
+    start = pl.multiple_of(b * bt, bt)
+    k = k_ref[pl.ds(start, span), :]
+    v = v_ref[pl.ds(start, span), :]
+    v_ext = jnp.concatenate([v, jnp.ones_like(v)], axis=1)
+    lo = jnp.concatenate([lo_ref[:, :1]] * CHAIN, axis=0)
+
+    def hide(s):
+        col = lax.broadcasted_iota(jnp.int32, s.shape, 1)
+        row = lax.broadcasted_iota(jnp.int32, s.shape, 0) % bt
+        return jnp.where((col + start >= lo) & (col <= row + halo), s, MASKED)
+
+    for g in range(heads // CHAIN):
+        q = q_ref[g * CHAIN : (g + 1) * CHAIN].reshape(rows, HD)
+        _, acc = absorb(hide(scores(q, k)), v_ext, m_ref[0, g][:, :1], acc_ref[0, g])
+        mixed = (acc[:, :HD] / acc[:, HD:]).astype(jnp.bfloat16)
+        for h in range(CHAIN):
+            at = (g * CHAIN + h) * HD
+            out_ref[:, at : at + HD] = mixed[h * bt : (h + 1) * bt]
+
+
+def attend_new(q, lo_tok, k, v, m, acc):
+    heads, tokens, _ = q.shape
+    blocks = tokens // BT
+    chains, rows = heads // CHAIN, CHAIN * BT
+    halo = k.shape[0] - tokens
+    whole = lambda b: (0, 0)
+    return pl.pallas_call(
+        functools.partial(new_kernel, halo),
+        out_shape=jax.ShapeDtypeStruct((tokens, heads * HD), jnp.bfloat16),
+        grid=(blocks,),
+        in_specs=[
+            pl.BlockSpec((heads, BT, HD), lambda b: (0, b, 0)),
+            pl.BlockSpec((BT, 128), lambda b: (b, 0)),
+            pl.BlockSpec(k.shape, whole),
+            pl.BlockSpec(v.shape, whole),
+            pl.BlockSpec((1, chains, rows, 128), lambda b: (b, 0, 0, 0)),
+            pl.BlockSpec((1, chains, rows, 2 * HD), lambda b: (b, 0, 0, 0)),
+        ],
+        out_specs=pl.BlockSpec((BT, heads * HD), lambda b: (b, 0)),
+        compiler_params=pltpu.CompilerParams(vmem_limit_bytes=40 * MIB),
+        cost_estimate=pl.CostEstimate(
+            flops=8 * heads * tokens * (halo + BT) * HD,
+            bytes_accessed=4 * tokens * heads * HD * 4,
+            transcendentals=heads * tokens * (halo + BT),
+        ),
+    )(q, lo_tok, k, v, m, acc)
+
+
+def out_kernel(ids_ref, *refs):
+    xs, ws = refs[:8], refs[8:13]
+    out_ref, x_buf, w_buf, x_sem, w_sem = refs[13:]
+    chip, core, z = ids_ref[0], ids_ref[1], ids_ref[2]
+    width = xs[0].shape[1]
+    rows = w_buf.shape[1] // 4
+    top = ws[3].shape[0]
+    for r in range(4):
+        near = ids_ref[2 + r] ^ z
+        for m in range(4):
+            to = w_buf.at[r, pl.ds(pl.multiple_of((chip ^ m) * rows, 128), rows)]
+            sem = w_sem.at[4 * r + m]
+            if m < 3:
+                src = ws[m].at[pl.ds(pl.multiple_of(near * rows, 128), rows)]
+                pltpu.make_async_copy(src, to, sem).start()
+            else:
+
+                @pl.when(near < 2)
+                def _():
+                    src = ws[3].at[pl.ds(pl.multiple_of(near * rows, 128), rows)]
+                    pltpu.make_async_copy(src, to, sem).start()
+
+                @pl.when(near >= 2)
+                def _():
+                    src = ws[4].at[pl.ds(pl.multiple_of(near * rows - top, 128), rows)]
+                    pltpu.make_async_copy(src, to, sem).start()
+
+        for s in range(2):
+            at = pl.multiple_of((core ^ s) * width, 128)
+            pltpu.make_async_copy(
+                xs[2 * r + s], x_buf.at[r, :, pl.ds(at, width)], x_sem.at[2 * r + s]
+            ).start()
+    acc = None
+    for r in range(4):
+        for m in range(4):
+            pltpu.make_async_copy(
+                ws[0].at[pl.ds(0, rows)], w_buf.at[r, pl.ds(0, rows)], w_sem.at[4 * r + m]
+            ).wait()
+        for s in range(2):
+            pltpu.make_async_copy(
+                xs[0], x_buf.at[r, :, pl.ds(0, width)], x_sem.at[2 * r + s]
+            ).wait()
+        term = jnp.dot(x_buf[r], w_buf[r], preferred_element_type=jnp.float32)
+        acc = term if acc is None else acc + term
+    out_ref[...] = acc.astype(jnp.bfloat16)
+
+
+def out_project(ids, xs, ws):
+    tokens, width = xs[0].shape
+    depth, cols = ws[0].shape
+    hbm = pl.BlockSpec(memory_space=pl.ANY)
+    return pl.pallas_call(
+        out_kernel,
+        out_shape=jax.ShapeDtypeStruct((tokens, cols), jnp.bfloat16),
+        in_specs=[pl.BlockSpec(memory_space=pltpu.SMEM)] + [hbm] * 13,
+        out_specs=pl.BlockSpec(memory_space=pltpu.VMEM),
+        scratch_shapes=[
+            pltpu.VMEM((4, tokens, 2 * width), jnp.bfloat16),
+            pltpu.VMEM((4, depth, cols), jnp.bfloat16),
+            pltpu.SemaphoreType.DMA((8,)),
+            pltpu.SemaphoreType.DMA((16,)),
+        ],
+        compiler_params=pltpu.CompilerParams(vmem_limit_bytes=40 * MIB),
+        cost_estimate=pl.CostEstimate(
+            flops=2 * tokens * 4 * depth * cols,
+            bytes_accessed=8 * depth * (tokens + cols),
+            transcendentals=0,
+        ),
+    )(ids, *xs, *ws)
+
+
+def per_device(
+    stream,
+    pending,
+    norm_gain,
+    w_query,
+    w_key,
+    w_value,
+    w_out,
+    prefix_keys,
+    prefix_values,
+    prefix_segments,
+    stretch_segments,
+    stretch_offset,
+):
+    tok, feat = stream.shape
+    chip_tok = 2 * tok
+    c = lax.axis_index("ctx")
+    z = lax.axis_index("tp")
+    chip, core = c // 2, c % 2
+    first = core == 0
+    depth = feat * N_TP
+
+    wide = stream.astype(jnp.float32)
+    gain = lax.dynamic_slice_in_dim(norm_gain, z * feat, feat, 0).astype(jnp.float32)
+    scaled = (wide * gain[None, :]).astype(jnp.bfloat16)
+    arrivals, parts, places = gather_steps(scaled, z)
+    ids = jnp.concatenate([jnp.stack([chip, core]), places]).astype(jnp.int32)
+    step1, step2, step3 = (none_of(*pair) for pair in arrivals)
+    xs = []
+    for part in parts:
+        xs += [part, swap(part, 1)]
+
+    def halves(w, width, base):
+        mine = lax.dynamic_slice_in_dim(w, base + core * width, width, 1)
+        theirs = lax.dynamic_slice_in_dim(w, base + (1 - core) * width, width, 1)
+        return mine, swap(theirs, 1)
+
+    def plane(own, other, zero_other, zero_far):
+        own_x, own_y = swap(own, 2), swap(own, 4)
+        late = after(other, zero_other)
+        other_x, other_y = swap(late, 2), swap(late, 4)
+        far_own = swap(after(own_x, zero_far), 4)
+        far_other = swap(after(other_y, zero_far), 2)
+        return own, other, own_x, other_x, own_y, other_y, far_own, far_other
+
+    q_heads = w_query.shape[1] // HD // 2
+    wq_parts = plane(*halves(w_query, q_heads * HD, 0), step1, step2)
+    kv_old = jnp.stack([prefix_keys, prefix_values])
+    old_own = lax.dynamic_index_in_dim(kv_old, 2 * z + core, 1, keepdims=False)
+    old_other = swap(lax.dynamic_index_in_dim(kv_old, 2 * z + 1 - core, 1, keepdims=False), 1)
+    old_parts = plane(old_own, old_other, step1, step2)
+    span = old_own.shape[1]
+    kv = jnp.zeros((2, N_CTX * span, HD), jnp.bfloat16)
+    for index, part in enumerate(old_parts):
+        from_ctx = ((chip ^ (index // 2)) * 2 + (core ^ (index % 2))) * span
+        kv = lax.dynamic_update_slice(kv, part, (0, from_ctx, 0))
+
+    piece_rows = w_out.shape[0] // 4
+
+    def piece(q):
+        return lax.dynamic_slice_in_dim(w_out, q * piece_rows, piece_rows, 0)
+
+    to_x, to_y = swap(piece(chip ^ 1), 2), swap(piece(chip ^ 2), 4)
+    to_far = swap(after(piece(chip ^ 3), step1), 6)
+    by_chip = jnp.stack([piece(chip), to_x, to_y, to_far])
+
+    def of_chip(q):
+        return lax.dynamic_index_in_dim(by_chip, q ^ chip, 0, keepdims=False)
+
+    pieces = [of_chip(z)]
+    for r in (1, 2, 3):
+        pieces.append(
+            lax.ppermute(after(of_chip(z ^ r), step3), "tp", [(i, i ^ r) for i in range(N_TP)])
+        )
+    moved = none_of(*pieces[1:])
+    block = jnp.concatenate(pieces, axis=0)
+    half = block.shape[0] // 2
+    wo_x, wo_y = swap(block, 2), swap(block, 4)
+    wo_parts = (block, wo_x, wo_y, swap(wo_x[:half], 4), swap(wo_y[half:], 2))
+
+    def share(place):
+        return lax.dynamic_slice_in_dim(pending[0], jnp.clip(place, 0, N_TP - 1) * feat, feat, 1)
+
+    up = hop_up(after(share(z + 3), step1), (0,))
+    down = hop_down(after(share(z - 3), step1), (0,))
+    up = hop_up(after(share(z + 2) + up, step2), (0, 1))
+    down = hop_down(after(share(z - 2) + down, step2), (0, 1))
+    up = hop_up(after(share(z + 1) + up, moved), (0, 1, 2))
+    down = hop_down(after(share(z - 1) + down, moved), (0, 1, 2))
+    pending_share = (
+        share(z).astype(jnp.float32) + up.astype(jnp.float32) + down.astype(jnp.float32)
+    )
+
+    squares = jnp.sum(wide * wide, axis=1)[None, :]
+    for r in (1, 2):
+        squares = squares + lax.ppermute(squares, "tp", [(i, i ^ r) for i in range(N_TP)])
+    factor = lax.rsqrt(squares[0] * (1.0 / depth) + NORM_EPSILON)
+
+    labels = jnp.arange(NTRAJ, dtype=jnp.int32)
+    counts = jnp.stack(
+        [
+            jnp.sum((prefix_segments[:, None] <= labels).astype(jnp.int32), axis=0),
+            jnp.sum((stretch_segments[:, None] < labels).astype(jnp.int32), axis=0),
+        ]
+    )
+    for bit in (1, 2, 4):
+        counts = counts + swap(counts, bit)
+
+    def of_chip_tokens(mine):
+        theirs = swap(mine, 1)
+        return jnp.where(
+            first, jnp.concatenate([mine, theirs], axis=0), jnp.concatenate([theirs, mine], axis=0)
+        )
+
+    factor = jnp.broadcast_to(of_chip_tokens(factor)[:, None], (chip_tok, 128))
+    segs = of_chip_tokens(stretch_segments)
+    onehot = (segs[:, None] == labels).astype(jnp.int32)
+    n_tok = jnp.sum(onehot * counts[0], axis=1)
+    lo_tok = jnp.sum(onehot * counts[1], axis=1) - chip * chip_tok + tok
+    blocked = n_tok.reshape(chip_tok // BT, BT)
+    bounds = jnp.stack([blocked[:, 0], blocked[:, -1]])
+    n_wide = jnp.broadcast_to(n_tok[:, None], (chip_tok, 128))
+    lo_wide = jnp.broadcast_to(lo_tok[:, None], (chip_tok, 128))
+
+    token_index = chip * chip_tok + jnp.arange(chip_tok, dtype=jnp.int32)
+    positions = stretch_offset[0].astype(jnp.float32) + token_index.astype(jnp.float32)
+    angles = positions[:, None] * inverse_freqs(HD)
+    cosine, sinus = jnp.cos(angles), jnp.sin(angles)
+    cosine = jnp.concatenate([cosine, cosine], axis=1)
+    sinus = jnp.concatenate([-sinus, sinus], axis=1)
+
+    scale = math.log2(math.e) / math.sqrt(HD)
+    q = project(ids, xs, wq_parts, factor, cosine, sinus, q_heads, q_heads, scale)
+    m, acc = attend_prefix(bounds, q, n_wide, kv)
+
+    mine_k, other_k = halves(w_key, HD, 2 * z * HD)
+    mine_v, other_v = halves(w_value, HD, 2 * z * HD)
+    wkv_parts = plane(
+        after(jnp.concatenate([mine_k, mine_v], axis=1), step3),
+        jnp.concatenate([other_k, other_v], axis=1),
+        step3,
+        step3,
+    )
+    kv_new = project(ids, xs, wkv_parts, factor, cosine, sinus, 2, 1, 1.0)
+    before = lax.ppermute(kv_new[:, tok:], "ctx", [(i, i + 2) for i in range(N_CTX - 2)])
+    k_near = jnp.concatenate([before[0], kv_new[0]], axis=0)
+    v_near = jnp.concatenate([before[1], kv_new[1]], axis=0)
+    attended = attend_new(q, lo_wide, k_near, v_near, m, acc)
+
+    _, heads_parts, _ = gather_steps(attended, z)
+    hs = []
+    for part in heads_parts:
+        hs += [part, swap(part, 1)]
+    projected = out_project(ids, hs, wo_parts)
+    mine = lax.dynamic_slice_in_dim(projected, core * tok, tok, 0)
+    theirs = swap(lax.dynamic_slice_in_dim(projected, (1 - core) * tok, tok, 0), 1)
+    head_share = jnp.where(
+        first,
+        jnp.concatenate([mine, theirs], axis=1),
+        jnp.concatenate([theirs, mine], axis=1),
+    ).astype(jnp.float32)
+    return (wide + (head_share + pending_share)).astype(jnp.bfloat16)
 
 
 def solution(mesh):
@@ -190,6 +702,11 @@
         P(),
     )
     out_specs = P("ctx", "tp")
+    small = mesh.shape["ctx"] == N_CTX and mesh.shape["tp"] == N_TP
     return jax.shard_map(
-        per_device, mesh=mesh, in_specs=in_specs, out_specs=out_specs, check_vma=False
-    )
+        per_device if small else per_device_any,
+        mesh=mesh,
+        in_specs=in_specs,
+        out_specs=out_specs,
+        check_vma=False,
+    )

time: 685 us -> 501 us (0.73)
  the two profiles are of different devices: /device:TPU:0 before, /device:TPU:6 now
where the time goes in v2:
time: 501 us; the launch traced here: 496 us
  waiting for transfers between devices  236 us (47%)
  starting transfers between devices  101 us (20%)
  Pallas kernels  71 us (14%)
  local copies, waits for them, and re-layouts  39.9 us (8%)
  other arithmetic  39.5 us (8%)
  between operations  7.94 us (2%)
    ppermute x43, waiting for transfers between devices, swap(): return lax.ppermute(x, 'ctx', [(c, c ^ bit) for c in range(N_CTX)])  117 us
    ppermute x9, waiting for transfers between devices, hop_up(): return lax.ppermute(v, 'tp', [(i, i + 1) for i in pairs])  44.1 us
    ppermute x9, waiting for transfers between devices, hop_down(): return lax.ppermute(v, 'tp', [(N_TP - 1 - i, N_TP - 2 - i) for i in pairs])  38.3 us
    pallas_call x1, Pallas kernels, attend_prefix(): pl.pallas_call(prefix_kernel, out_shape=(jax.ShapeDtypeStruct((blocks, ch...  37.3 us
    ppermute x3, starting transfers between devices, per_device(): lax.ppermute(after(of_chip(z ^ r), step3), 'tp', [(i, i ^ r) for i in ran...  34.4 us
    ppermute x3, waiting for transfers between devices, per_device(): lax.ppermute(after(of_chip(z ^ r), step3), 'tp', [(i, i ^ r) for i in ran...  32.3 us
    ppermute x9, starting transfers between devices, hop_up(): return lax.ppermute(v, 'tp', [(i, i + 1) for i in pairs])  27.7 us
    ppermute x43, starting transfers between devices, swap(): return lax.ppermute(x, 'ctx', [(c, c ^ bit) for c in range(N_CTX)])  21.9 us
  transfers between devices with their start and end apart: 67, of which 31 were waited for; matrix products, arithmetic and copies ran while one was open for 13% of the time, Pallas kernels for 14%

profile of v2, /device:TPU:6, one launch (start us, length us, event | category | flops | bytes accessed | tf_op | source)
XLA Modules:
  0.0 495.8 jit_solution(7096894245371509675)
XLA Ops:
  25.4 14.5 %collective-permute-done.2 = bf16[384,2048]{1,0:T(8,128)(2,1)} collective-permute-done((bf16[384,2048]{1,0:T(8,128)(2,1)S(1)}, bf16[384,2048]{1,0:T(8,128)(2,1)}, u32[]{:S(2)}, u32[]{:S(2)}) %collective-permute-start.2) | collective-permute-done | bytes 1572896 | tf_op jit(solution)/shard_map/ppermute | solution.py:179
  73.0 11.0 %collective-permute-done.4 = bf16[384,2048]{1,0:T(8,128)(2,1)} collective-permute-done((bf16[384,2048]{1,0:T(8,128)(2,1)}, bf16[384,2048]{1,0:T(8,128)(2,1)}, u32[]{:S(2)}, u32[]{:S(2)}) %collective-permute-start.4) | collective-permute-done | bytes 1572896 | tf_op jit(solution)/shard_map/ppermute | solution.py:183
  88.8 13.4 %collective-permute-done.35 = bf16[2,768,128]{2,1,0:T(8,128)(2,1)S(1)} collective-permute-done((bf16[2,768,128]{2,1,0:T(8,128)(2,1)S(1)}, bf16[2,768,128]{2,1,0:T(8,128)(2,1)S(1)}, u32[]{:S(2)}, u32[]{:S(2)}) %collective-permute-start.35) | collective-permute-done | bytes 393248 | tf_op jit(solution)/shard_map/ppermute | solution.py:175
  116.0 8.1 %collective-permute-done.37 = bf16[2,768,128]{2,1,0:T(8,128)(2,1)S(1)} collective-permute-done((bf16[2,768,128]{2,1,0:T(8,128)(2,1)S(1)}, bf16[2,768,128]{2,1,0:T(8,128)(2,1)S(1)}, u32[]{:S(2)}, u32[]{:S(2)}) %collective-permute-start.37) | collective-permute-done | bytes 393248 | tf_op jit(solution)/shard_map/ppermute | solution.py:175
  126.9 8.1 %collective-permute-done.7 = bf16[384,2048]{1,0:T(8,128)(2,1)S(1)} collective-permute-done((bf16[384,2048]{1,0:T(8,128)(2,1)}, bf16[384,2048]{1,0:T(8,128)(2,1)S(1)}, u32[]{:S(2)}, u32[]{:S(2)}) %collective-permute-start.7) | collective-permute-done | bytes 1572896 | tf_op jit(solution)/shard_map/ppermute | solution.py:183
  140.2 28.5 %collective-permute-done.51 = bf16[256,1024]{1,0:T(8,128)(2,1)S(1)} collective-permute-done((bf16[256,1024]{1,0:T(8,128)(2,1)S(1)}, bf16[256,1024]{1,0:T(8,128)(2,1)S(1)}, u32[]{:S(2)}, u32[]{:S(2)}) %collective-permute-start.51) | collective-permute-done | bytes 524320 | tf_op jit(solution)/shard_map/ppermute | solution.py:175
  179.0 9.4 %collective-permute-done.29.refs_13_ = bf16[1024,256]{1,0:T(8,128)(2,1)S(1)} collective-permute-done((bf16[1024,256]{1,0:T(8,128)(2,1)S(1)}, bf16[1024,256]{1,0:T(8,128)(2,1)S(1)}, u32[]{:S(2)}, u32[]{:S(2)}) %collective-permute-start.29) | collective-permute-done | bytes 524320 | tf_op jit(solution)/shard_map/ppermute | solution.py:175
  188.4 29.8 %collective-permute-start.55 = (bf16[256,1024]{1,0:T(8,128)(2,1)S(1)}, bf16[256,1024]{1,0:T(8,128)(2,1)S(1)}, u32[]{:S(2)}, u32[]{:S(2)}) collective-permute-start(bf16[256,1024]{1,0:T(8,128)(2,1)S(1)} %get-tuple-element.24), channel_id=1, source_target_pairs={{0,3},{1,2},{2,1},{3,0},{4,7},{5,6},{6,5},{7,4},{8,11},{9,10},{10,... | collective-permute-start | bytes 1572872 | tf_op jit(solution)/shard_map/ppermute | solution.py:597
  223.0 8.0 %collective-permute-done.55 = bf16[256,1024]{1,0:T(8,128)(2,1)S(1)} collective-permute-done((bf16[256,1024]{1,0:T(8,128)(2,1)S(1)}, bf16[256,1024]{1,0:T(8,128)(2,1)S(1)}, u32[]{:S(2)}, u32[]{:S(2)}) %collective-permute-start.55) | collective-permute-done | bytes 524320 | tf_op jit(solution)/shard_map/ppermute | solution.py:597
  231.0 24.3 %collective-permute-done.54 = bf16[256,1024]{1,0:T(8,128)(2,1)S(1)} collective-permute-done((bf16[256,1024]{1,0:T(8,128)(2,1)S(1)}, bf16[256,1024]{1,0:T(8,128)(2,1)S(1)}, u32[]{:S(2)}, u32[]{:S(2)}) %collective-permute-start.54) | collective-permute-done | bytes 524320 | tf_op jit(solution)/shard_map/ppermute | solution.py:597
  260.1 10.1 %collective-permute-done.30.refs_14_ = bf16[1024,256]{1,0:T(8,128)(2,1)S(1)} collective-permute-done((bf16[1024,256]{1,0:T(8,128)(2,1)S(1)}, bf16[1024,256]{1,0:T(8,128)(2,1)S(1)}, u32[]{:S(2)}, u32[]{:S(2)}) %collective-permute-start.30) | collective-permute-done | bytes 524320 | tf_op jit(solution)/shard_map/ppermute | solution.py:175
  282.0 9.1 %shard_map.119 = bf16[2,768,128]{2,1,0:T(8,128)(2,1)S(1)} custom-call(s32[6]{0:T(128)S(1)} %concatenate.58.ids_ref, bf16[384,2048]{1,0:T(8,128)(2,1)S(1)} %get-tuple-element.42.refs_0_, bf16[384,2048]{1,0:T(8,128)(2,1)S(1)} %collective-permute-done.refs_1_, bf16[384,2048]{1,0:T(8,128)(2,1)S(1)} %get-tuple-element.22.refs_2_, ...), custom_call_target="tpu_custom_call" | custom-call | flops 3221225472 | bytes 16777216 | tf_op jit(solution)/shard_map/pallas_call | solution.py:272
  296.4 8.9 %collective-permute-done.16.refs_15_ = bf16[1024,512]{1,0:T(8,128)(2,1)S(1)} collective-permute-done((bf16[1024,512]{1,0:T(8,128)(2,1)}, bf16[1024,512]{1,0:T(8,128)(2,1)S(1)}, u32[]{:S(2)}, u32[]{:S(2)}) %collective-permute-start.16) | collective-permute-done | bytes 1048608 | tf_op jit(solution)/shard_map/ppermute | solution.py:175
  306.6 8.5 %collective-permute-done.15.refs_14_ = bf16[1024,512]{1,0:T(8,128)(2,1)S(1)} collective-permute-done((bf16[1024,512]{1,0:T(8,128)(2,1)}, bf16[1024,512]{1,0:T(8,128)(2,1)S(1)}, u32[]{:S(2)}, u32[]{:S(2)}) %collective-permute-start.15) | collective-permute-done | bytes 1048608 | tf_op jit(solution)/shard_map/ppermute | solution.py:175
  315.1 9.3 %shard_map.118.q_ref = bf16[4,768,128]{2,1,0:T(8,128)(2,1)S(1)} custom-call(s32[6]{0:T(128)S(1)} %concatenate.58.ids_ref, bf16[384,2048]{1,0:T(8,128)(2,1)S(1)} %get-tuple-element.42.refs_0_, bf16[384,2048]{1,0:T(8,128)(2,1)S(1)} %collective-permute-done.refs_1_, bf16[384,2048]{1,0:T(8,128)(2,1)} %copy-done.1, bf16[384,2048]{1,0:T(8,128)(2,1)} %copy-done.2, ...), custom_call_target="tpu_custom_call" | custom-call | flops 6442450944 | bytes 20971520 | tf_op jit(solution)/shard_map/pallas_call | solution.py:272
  324.6 37.3 %shard_map.120 = (f32[3,2,512,128]{3,2,1,0:T(8,128)S(1)}, f32[3,2,512,256]{3,2,1,0:T(8,128)S(1)}) custom-call(s32[2,3]{1,0:T(2,128)S(1)} %pad_add_fusion.1.bound_ref, bf16[4,768,128]{2,1,0:T(8,128)(2,1)S(1)} %shard_map.118.q_ref, s32[768,128]{1,0:T(8,128)S(1)} %broadcast_in_dim.13.n_ref, bf16[2,6144,128]{2,1,0:T(8,128)(2,1)} %constant_dynamic-update-slice_fusion.kv_ref), custom_call_target="tpu_custom_call" | custom-call | flops 19327352832 | bytes 3145728 | tf_op jit(solution)/shard_map/pallas_call | solution.py:367
  370.9 10.3 %collective-permute-done.42 = bf16[768,512]{1,0:T(8,128)(2,1)} collective-permute-done((bf16[768,512]{1,0:T(8,128)(2,1)}, bf16[768,512]{1,0:T(8,128)(2,1)}, u32[]{:S(2)}, u32[]{:S(2)}) %collective-permute-start.42) | collective-permute-done | bytes 786464 | tf_op jit(solution)/shard_map/ppermute | solution.py:179
  381.9 5.3 %collective-permute-done.41 = bf16[768,512]{1,0:T(8,128)(2,1)} collective-permute-done((bf16[768,512]{1,0:T(8,128)(2,1)}, bf16[768,512]{1,0:T(8,128)(2,1)}, u32[]{:S(2)}, u32[]{:S(2)}) %collective-permute-start.41) | collective-permute-done | bytes 786464 | tf_op jit(solution)/shard_map/ppermute | solution.py:183
  399.2 6.0 %collective-permute-done.44 = bf16[768,512]{1,0:T(8,128)(2,1)S(1)} collective-permute-done((bf16[768,512]{1,0:T(8,128)(2,1)}, bf16[768,512]{1,0:T(8,128)(2,1)S(1)}, u32[]{:S(2)}, u32[]{:S(2)}) %collective-permute-start.44) | collective-permute-done | bytes 786464 | tf_op jit(solution)/shard_map/ppermute | solution.py:183
  406.4 7.2 %collective-permute-done.56.refs_9_ = bf16[1024,1024]{1,0:T(8,128)(2,1)S(1)} collective-permute-done((bf16[1024,1024]{1,0:T(8,128)(2,1)}, bf16[1024,1024]{1,0:T(8,128)(2,1)S(1)}, u32[]{:S(2)}, u32[]{:S(2)}) %collective-permute-start.56) | collective-permute-done | bytes 2097184 | tf_op jit(solution)/shard_map/ppermute | solution.py:175
  432.2 5.6 %fusion.8 = (bf16[384,2048]{1,0:T(8,128)(2,1)}, bf16[384,2048]{1,0:T(8,128)(2,1)}) fusion(bf16[384,2048]{1,0:T(8,128)(2,1)S(1)} %copy-done.19, bf16[1,384,8192]{2,1,0:T(8,128)(2,1)} %param.13, s32[]{:T(128)S(6)} %select_n.285, bf16[]{:T(256)} %bitcast.34, bf16[384,2048]{1,0:T(8,128)(2,1)} %copy-done.20, s32[]{:T(128)S(6)} %select_n.288), kind=kLoop, calls=%fused_computation.23 | loop fusion | flops 8650752 | bytes 9437194 | tf_op jit(solution)/shard_map/add | solution.py:194
  443.0 9.5 %collective-permute-start.63 = (bf16[384,2048]{1,0:T(8,128)(2,1)}, bf16[384,2048]{1,0:T(8,128)(2,1)}, u32[]{:S(2)}, u32[]{:S(2)}) collective-permute-start(bf16[384,2048]{1,0:T(8,128)(2,1)} %get-tuple-element.15), channel_id=1, source_target_pairs={{0,1},{1,2},{2,3},{4,5},{5,6},{6,7},{8,9},{9,10},{10,11},{12,13},{... | collective-permute-start | bytes 4718600 | tf_op jit(solution)/shard_map/ppermute | solution.py:179
  456.6 10.2 %shard_map.122 = bf16[768,1024]{1,0:T(8,128)(2,1)S(1)} custom-call(s32[6]{0:T(128)S(1)} %concatenate.58.ids_ref, bf16[768,512]{1,0:T(8,128)(2,1)} %shard_map.121.refs_0_, bf16[768,512]{1,0:T(8,128)(2,1)S(1)} %copy-done.6, bf16[768,512]{1,0:T(8,128)(2,1)S(1)} %get-tuple-element.40.refs_2_, bf16[768,512]{1,0:T(8,128)(2,1)} %collective-permute-done.43.refs_3_, ...), custom_call_target="tpu_custom_call" | custom-call | flops 6442450944 | bytes 14680064 | tf_op jit(solution)/shard_map/pallas_call | solution.py:505
  468.1 17.9 %collective-permute-done.63 = bf16[384,2048]{1,0:T(8,128)(2,1)} collective-permute-done((bf16[384,2048]{1,0:T(8,128)(2,1)}, bf16[384,2048]{1,0:T(8,128)(2,1)}, u32[]{:S(2)}, u32[]{:S(2)}) %collective-permute-start.63) | collective-permute-done | bytes 1572896 | tf_op jit(solution)/shard_map/ppermute | solution.py:179
  (263 shorter events, 177.5 us)
Async XLA Ops:
  7.4 39.7 %collective-permute-start.1 = (bf16[384,2048]{1,0:T(8,128)(2,1)S(1)}, bf16[384,2048]{1,0:T(8,128)(2,1)}, u32[]{:S(2)}, u32[]{:S(2)}) collective-permute-start(bf16[384,2048]{1,0:T(8,128)(2,1)S(1)} %get-tuple-element.42.refs_0_), channel_id=1, source_target_pairs={{3,2},{2,1},{1,0},{7,6},{6,5},{5,4},{11,10},{10,9},{9,8},{15,14},{... | collective-permute-start | bytes 4718600 | tf_op jit(solution)/shard_map/ppermute | solution.py:183
  8.7 47.0 %collective-permute-start.20 = (s32[384]{0:T(512)S(1)}, s32[384]{0:T(512)S(1)}, u32[]{:S(2)}, u32[]{:S(2)}) collective-permute-start(s32[384]{0:T(512)S(1)} %copy-done.26), channel_id=1, source_target_pairs={{0,4},{4,0},{8,12},{12,8},{16,20},{20,16},{24,28},{28,24},{1,5},{5... | collective-permute-start | bytes 4616 | tf_op jit(solution)/shard_map/ppermute | solution.py:175
  9.0 39.3 %collective-permute-start.21 = (s32[2,16]{1,0:T(2,128)S(1)}, s32[2,16]{1,0:T(2,128)S(1)}, u32[]{:S(2)}, u32[]{:S(2)}) collective-permute-start(s32[2,16]{1,0:T(2,128)S(1)} %pad_add_fusion), channel_id=1, source_target_pairs={{0,4},{4,0},{8,12},{12,8},{16,20},{20,16},{24,28},{28,24},{1,5},{5... | collective-permute-start | bytes 392 | tf_op jit(solution)/shard_map/ppermute | solution.py:175
  65.8 49.6 %collective-permute-start = (bf16[384,2048]{1,0:T(8,128)(2,1)S(1)}, bf16[384,2048]{1,0:T(8,128)(2,1)S(1)}, u32[]{:S(2)}, u32[]{:S(2)}) collective-permute-start(bf16[384,2048]{1,0:T(8,128)(2,1)S(1)} %get-tuple-element.42.refs_0_), channel_id=1, source_target_pairs={{0,4},{4,0},{8,12},{12,8},{16,20},{20,16},{24,28},{28,24},{1,5},{5... | collective-permute-start | bytes 4718600 | tf_op jit(solution)/shard_map/ppermute | solution.py:175
  69.3 43.0 %collective-permute-start.11 = (bf16[1024,512]{1,0:T(8,128)(2,1)S(1)}, bf16[1024,512]{1,0:T(8,128)(2,1)S(1)}, u32[]{:S(2)}, u32[]{:S(2)}) collective-permute-start(bf16[1024,512]{1,0:T(8,128)(2,1)S(1)} %get-tuple-element.32.refs_8_), channel_id=1, source_target_pairs={{0,8},{4,12},{8,0},{12,4},{16,24},{20,28},{24,16},{28,20},{1,9},{5... | collective-permute-start | bytes 3145736 | tf_op jit(solution)/shard_map/ppermute | solution.py:175
  69.9 55.0 %collective-permute-start.8 = (bf16[384,2048]{1,0:T(8,128)(2,1)}, bf16[384,2048]{1,0:T(8,128)(2,1)S(1)}, u32[]{:S(2)}, u32[]{:S(2)}) collective-permute-start(bf16[384,2048]{1,0:T(8,128)(2,1)} %collective-permute-done.5), channel_id=1, source_target_pairs={{2,3},{6,7},{10,11},{14,15},{18,19},{22,23},{26,27},{30,31}} | collective-permute-start | bytes 4718600 | tf_op jit(solution)/shard_map/ppermute | solution.py:179
  84.0 51.0 %collective-permute-start.7 = (bf16[384,2048]{1,0:T(8,128)(2,1)}, bf16[384,2048]{1,0:T(8,128)(2,1)S(1)}, u32[]{:S(2)}, u32[]{:S(2)}) collective-permute-start(bf16[384,2048]{1,0:T(8,128)(2,1)} %collective-permute-done.4), channel_id=1, source_target_pairs={{1,0},{5,4},{9,8},{13,12},{17,16},{21,20},{25,24},{29,28}} | collective-permute-start | bytes 4718600 | tf_op jit(solution)/shard_map/ppermute | solution.py:183
  112.3 57.0 %collective-permute-start.14 = (bf16[1024,512]{1,0:T(8,128)(2,1)}, bf16[1024,512]{1,0:T(8,128)(2,1)S(1)}, u32[]{:S(2)}, u32[]{:S(2)}) collective-permute-start(bf16[1024,512]{1,0:T(8,128)(2,1)} %broadcast_add_fusion.2), channel_id=1, source_target_pairs={{0,16},{4,20},{8,24},{12,28},{16,0},{20,4},{24,8},{28,12},{1,17},{... | collective-permute-start | bytes 3145736 | tf_op jit(solution)/shard_map/ppermute | solution.py:175
  124.9 43.8 %collective-permute-start.51 = (bf16[256,1024]{1,0:T(8,128)(2,1)S(1)}, bf16[256,1024]{1,0:T(8,128)(2,1)S(1)}, u32[]{:S(2)}, u32[]{:S(2)}) collective-permute-start(bf16[256,1024]{1,0:T(8,128)(2,1)S(1)} %get-tuple-element.36), channel_id=1, source_target_pairs={{0,16},{4,20},{8,24},{12,28},{16,0},{20,4},{24,8},{28,12},{1,17},{... | collective-permute-start | bytes 1572872 | tf_op jit(solution)/shard_map/ppermute | solution.py:175
  135.0 43.4 %collective-permute-start.6 = (bf16[384,2048]{1,0:T(8,128)(2,1)S(1)}, bf16[384,2048]{1,0:T(8,128)(2,1)S(1)}, u32[]{:S(2)}, u32[]{:S(2)}) collective-permute-start(bf16[384,2048]{1,0:T(8,128)(2,1)S(1)} %broadcast_select_fusion.refs_4_), channel_id=1, source_target_pairs={{0,4},{4,0},{8,12},{12,8},{16,20},{20,16},{24,28},{28,24},{1,5},{5... | collective-permute-start | bytes 4718600 | tf_op jit(solution)/shard_map/ppermute | solution.py:175
  169.3 48.9 %collective-permute-start.27 = (bf16[1024,256]{1,0:T(8,128)(2,1)S(1)}, bf16[1024,256]{1,0:T(8,128)(2,1)S(1)}, u32[]{:S(2)}, u32[]{:S(2)}) collective-permute-start(bf16[1024,256]{1,0:T(8,128)(2,1)S(1)} %broadcast_add_fusion.5), channel_id=1, source_target_pairs={{0,8},{4,12},{8,0},{12,4},{16,24},{20,28},{24,16},{28,20},{1,9},{5... | collective-permute-start | bytes 1572872 | tf_op jit(solution)/shard_map/ppermute | solution.py:175
  177.2 93.6 %collective-permute-start.9 = (bf16[384,2048]{1,0:T(8,128)(2,1)S(1)}, bf16[384,2048]{1,0:T(8,128)(2,1)S(1)}, u32[]{:S(2)}, u32[]{:S(2)}) collective-permute-start(bf16[384,2048]{1,0:T(8,128)(2,1)S(1)} %get-tuple-element.21.refs_6_), channel_id=1, source_target_pairs={{0,4},{4,0},{8,12},{12,8},{16,20},{20,16},{24,28},{28,24},{1,5},{5... | collective-permute-start | bytes 4718600 | tf_op jit(solution)/shard_map/ppermute | solution.py:175
  177.6 40.6 %collective-permute-start.26 = (bf16[1024,256]{1,0:T(8,128)(2,1)S(1)}, bf16[1024,256]{1,0:T(8,128)(2,1)S(1)}, u32[]{:S(2)}, u32[]{:S(2)}) collective-permute-start(bf16[1024,256]{1,0:T(8,128)(2,1)S(1)} %maximum_add_fusion.refs_8_), channel_id=1, source_target_pairs={{0,8},{4,12},{8,0},{12,4},{16,24},{20,28},{24,16},{28,20},{1,9},{5... | collective-permute-start | bytes 1572872 | tf_op jit(solution)/shard_map/ppermute | solution.py:175
  178.4 40.0 %collective-permute-start.28 = (bf16[1024,256]{1,0:T(8,128)(2,1)S(1)}, bf16[1024,256]{1,0:T(8,128)(2,1)S(1)}, u32[]{:S(2)}, u32[]{:S(2)}) collective-permute-start(bf16[1024,256]{1,0:T(8,128)(2,1)S(1)} %maximum_add_fusion.refs_8_), channel_id=1, source_target_pairs={{0,16},{4,20},{8,24},{12,28},{16,0},{20,4},{24,8},{28,12},{1,17},{... | collective-permute-start | bytes 1572872 | tf_op jit(solution)/shard_map/ppermute | solution.py:175
  188.4 42.6 %collective-permute-start.55 = (bf16[256,1024]{1,0:T(8,128)(2,1)S(1)}, bf16[256,1024]{1,0:T(8,128)(2,1)S(1)}, u32[]{:S(2)}, u32[]{:S(2)}) collective-permute-start(bf16[256,1024]{1,0:T(8,128)(2,1)S(1)} %get-tuple-element.24), channel_id=1, source_target_pairs={{0,3},{1,2},{2,1},{3,0},{4,7},{5,6},{6,5},{7,4},{8,11},{9,10},{10,... | collective-permute-start | bytes 1572872 | tf_op jit(solution)/shard_map/ppermute | solution.py:597
  218.3 61.1 %collective-permute-start.3 = (bf16[384,2048]{1,0:T(8,128)(2,1)S(1)}, bf16[384,2048]{1,0:T(8,128)(2,1)S(1)}, u32[]{:S(2)}, u32[]{:S(2)}) collective-permute-start(bf16[384,2048]{1,0:T(8,128)(2,1)S(1)} %get-tuple-element.22.refs_2_), channel_id=1, source_target_pairs={{0,4},{4,0},{8,12},{12,8},{16,20},{20,16},{24,28},{28,24},{1,5},{5... | collective-permute-start | bytes 4718600 | tf_op jit(solution)/shard_map/ppermute | solution.py:175
  218.4 41.1 %collective-permute-start.53 = (bf16[256,1024]{1,0:T(8,128)(2,1)S(1)}, bf16[256,1024]{1,0:T(8,128)(2,1)S(1)}, u32[]{:S(2)}, u32[]{:S(2)}) collective-permute-start(bf16[256,1024]{1,0:T(8,128)(2,1)S(1)} %get-tuple-element.26), channel_id=1, source_target_pairs={{0,1},{1,0},{2,3},{3,2},{4,5},{5,4},{6,7},{7,6},{8,9},{9,8},{10,11... | collective-permute-start | bytes 1572872 | tf_op jit(solution)/shard_map/ppermute | solution.py:597
  271.9 43.2 %collective-permute-start.15 = (bf16[1024,512]{1,0:T(8,128)(2,1)}, bf16[1024,512]{1,0:T(8,128)(2,1)S(1)}, u32[]{:S(2)}, u32[]{:S(2)}) collective-permute-start(bf16[1024,512]{1,0:T(8,128)(2,1)} %broadcast_add_fusion.1), channel_id=1, source_target_pairs={{0,16},{4,20},{8,24},{12,28},{16,0},{20,4},{24,8},{28,12},{1,17},{... | collective-permute-start | bytes 3145736 | tf_op jit(solution)/shard_map/ppermute | solution.py:175
  279.4 91.4 %collective-permute-start.61 = (bf16[384,2048]{1,0:T(8,128)(2,1)}, bf16[384,2048]{1,0:T(8,128)(2,1)}, u32[]{:S(2)}, u32[]{:S(2)}) collective-permute-start(bf16[384,2048]{1,0:T(8,128)(2,1)} %get-tuple-element.19), channel_id=1, source_target_pairs={{0,1},{4,5},{8,9},{12,13},{16,17},{20,21},{24,25},{28,29}} | collective-permute-start | bytes 4718600 | tf_op jit(solution)/shard_map/ppermute | solution.py:179
  292.7 95.9 %collective-permute-start.64 = (bf16[384,2048]{1,0:T(8,128)(2,1)}, bf16[384,2048]{1,0:T(8,128)(2,1)}, u32[]{:S(2)}, u32[]{:S(2)}) collective-permute-start(bf16[384,2048]{1,0:T(8,128)(2,1)} %get-tuple-element.20), channel_id=1, source_target_pairs={{3,2},{7,6},{11,10},{15,14},{19,18},{23,22},{27,26},{31,30}} | collective-permute-start | bytes 4718600 | tf_op jit(solution)/shard_map/ppermute | solution.py:183
  294.5 103.2 %collective-permute-start.57 = (bf16[1024,1024]{1,0:T(8,128)(2,1)}, bf16[1024,1024]{1,0:T(8,128)(2,1)}, u32[]{:S(2)}, u32[]{:S(2)}) collective-permute-start(bf16[1024,1024]{1,0:T(8,128)(2,1)} %pad_maximum_fusion.1.refs_8_), channel_id=1, source_target_pairs={{0,16},{4,20},{8,24},{12,28},{16,0},{20,4},{24,8},{28,12},{1,17},{... | collective-permute-start | bytes 6291464 | tf_op jit(solution)/shard_map/ppermute | solution.py:175
  305.3 56.7 %collective-permute-start.32 = (bf16[2,384,128]{2,1,0:T(8,128)(2,1)S(1)}, bf16[2,384,128]{2,1,0:T(8,128)(2,1)S(1)}, u32[]{:S(2)}, u32[]{:S(2)}) collective-permute-start(bf16[2,384,128]{2,1,0:T(8,128)(2,1)S(1)} %slice.86), channel_id=1, source_target_pairs={{0,8},{4,12},{8,16},{12,20},{16,24},{20,28},{1,9},{5,13},{9,17},{1... | collective-permute-start | bytes 589832 | tf_op jit(solution)/shard_map/ppermute | solution.py:669
  370.8 42.9 %collective-permute-start.56 = (bf16[1024,1024]{1,0:T(8,128)(2,1)}, bf16[1024,1024]{1,0:T(8,128)(2,1)S(1)}, u32[]{:S(2)}, u32[]{:S(2)}) collective-permute-start(bf16[1024,1024]{1,0:T(8,128)(2,1)} %pad_maximum_fusion.1.refs_8_), channel_id=1, source_target_pairs={{0,8},{4,12},{8,0},{12,4},{16,24},{20,28},{24,16},{28,20},{1,9},{5... | collective-permute-start | bytes 6291464 | tf_op jit(solution)/shard_map/ppermute | solution.py:175
  443.0 43.0 %collective-permute-start.63 = (bf16[384,2048]{1,0:T(8,128)(2,1)}, bf16[384,2048]{1,0:T(8,128)(2,1)}, u32[]{:S(2)}, u32[]{:S(2)}) collective-permute-start(bf16[384,2048]{1,0:T(8,128)(2,1)} %get-tuple-element.15), channel_id=1, source_target_pairs={{0,1},{1,2},{2,3},{4,5},{5,6},{6,7},{8,9},{9,10},{10,11},{12,13},{... | collective-permute-start | bytes 4718600 | tf_op jit(solution)/shard_map/ppermute | solution.py:179
  (73 other events, 1777.0 us)

commit v3 on v2

--- a/solution.py
+++ b/solution.py
@@ -194,10 +194,8 @@
     return x + zero.astype(x.dtype)
 
 
-def gather_steps(x, z):
-    u1, d1 = hop_up(x, (0, 1, 2)), hop_down(x, (0, 1, 2))
-    u2, d2 = hop_up(u1, (1, 2)), hop_down(d1, (1, 2))
-    u3, d3 = hop_up(u2, (2,)), hop_down(d2, (2,))
+def line_parts(z, one, two, three):
+    (u1, d1), (u2, d2), (u3, d3) = one, two, three
     low = z < 2
     a = jnp.where(low, d1, u1)
     b = jnp.where(low, d2, u2)
@@ -206,7 +204,7 @@
     places = jnp.stack(
         [z, jnp.where(low, z + 1, z - 1), jnp.where(low, z + 2, z - 2), jnp.where(z % 2 == 1, 0, 3)]
     )
-    return ((u1, d1), (u2, d2), (u3, d3)), (x, a, b, c), places
+    return (a, b, c), places
 
 
 def rotated(v, cosine, sinus):
@@ -240,15 +238,20 @@
 
                 @pl.when(part == m)
                 def _():
-                    pltpu.make_async_copy(ws[2 * m + h], w_buf.at[at], w_sem.at[at]).start()
+                    src = ws[2 * m + h].at[pl.ds(0, half)]
+                    pltpu.make_async_copy(src, w_buf.at[at], w_sem.at[at]).start()
 
             for s, rows in ((0, mine), (1, theirs)):
+                src = xs[2 * r + s]
+                skip = tok if src.shape[0] > tok and r == 1 else 0
                 pltpu.make_async_copy(
-                    xs[2 * r + s].at[:, cols], x_buf.at[at, pl.ds(rows, tok)], x_sem.at[2 * at + s]
+                    src.at[pl.ds(skip, tok), cols],
+                    x_buf.at[at, pl.ds(rows, tok)],
+                    x_sem.at[2 * at + s],
                 ).start()
     acc = None
     for at in range(8):
-        pltpu.make_async_copy(ws[0], w_buf.at[at], w_sem.at[at]).wait()
+        pltpu.make_async_copy(ws[0].at[pl.ds(0, half)], w_buf.at[at], w_sem.at[at]).wait()
         for s in range(2):
             pltpu.make_async_copy(
                 xs[0].at[:, pl.ds(0, half)], x_buf.at[at, pl.ds(0, tok)], x_sem.at[2 * at + s]
@@ -359,8 +362,8 @@
     acc_out[0] = acc_ref[...]
 
 
-def attend_prefix(bounds, q, n_tok, kv):
-    heads, tokens, _ = q.shape
+def attend_prefix(bounds, q, group, n_tok, kv):
+    heads, tokens = CHAIN, q.shape[1]
     blocks = tokens // BT
     chains, rows = heads // CHAIN, CHAIN * BT
     keys = kv.shape[1]
@@ -374,7 +377,7 @@
             num_scalar_prefetch=1,
             grid=(blocks,),
             in_specs=[
-                pl.BlockSpec((heads, BT, HD), lambda b, *_: (0, b, 0)),
+                pl.BlockSpec((heads, BT, HD), lambda b, *_: (group, b, 0)),
                 pl.BlockSpec((BT, 128), lambda b, *_: (b, 0)),
                 pl.BlockSpec((2, keys, HD), lambda b, *_: (0, 0, 0)),
             ],
@@ -391,14 +394,13 @@
         ),
         compiler_params=pltpu.CompilerParams(vmem_limit_bytes=40 * MIB),
         cost_estimate=pl.CostEstimate(
-            flops=8 * heads * tokens * keys * HD,
-            bytes_accessed=4 * keys * HD,
-            transcendentals=heads * tokens * keys,
+            flops=heads * tokens * HD, bytes_accessed=4 * keys * HD, transcendentals=0
         ),
     )(bounds, q, n_tok, kv)
 
 
-def new_kernel(halo, q_ref, lo_ref, k_ref, v_ref, m_ref, acc_ref, out_ref):
+def new_kernel(halo, q_ref, lo_ref, k_ref, v_ref, *refs):
+    states, out_ref = refs[:-1], refs[-1]
     b = pl.program_id(0)
     heads, bt = q_ref.shape[0], q_ref.shape[1]
     rows = CHAIN * bt
@@ -416,14 +418,16 @@
 
     for g in range(heads // CHAIN):
         q = q_ref[g * CHAIN : (g + 1) * CHAIN].reshape(rows, HD)
-        _, acc = absorb(hide(scores(q, k)), v_ext, m_ref[0, g][:, :1], acc_ref[0, g])
+        _, acc = absorb(
+            hide(scores(q, k)), v_ext, states[2 * g][0, 0][:, :1], states[2 * g + 1][0, 0]
+        )
         mixed = (acc[:, :HD] / acc[:, HD:]).astype(jnp.bfloat16)
         for h in range(CHAIN):
             at = (g * CHAIN + h) * HD
             out_ref[:, at : at + HD] = mixed[h * bt : (h + 1) * bt]
 
 
-def attend_new(q, lo_tok, k, v, m, acc):
+def attend_new(q, lo_tok, k, v, states):
     heads, tokens, _ = q.shape
     blocks = tokens // BT
     chains, rows = heads // CHAIN, CHAIN * BT
@@ -438,17 +442,18 @@
             pl.BlockSpec((BT, 128), lambda b: (b, 0)),
             pl.BlockSpec(k.shape, whole),
             pl.BlockSpec(v.shape, whole),
-            pl.BlockSpec((1, chains, rows, 128), lambda b: (b, 0, 0, 0)),
-            pl.BlockSpec((1, chains, rows, 2 * HD), lambda b: (b, 0, 0, 0)),
-        ],
+        ]
+        + [
+            pl.BlockSpec((1, 1, rows, 128), lambda b: (b, 0, 0, 0)),
+            pl.BlockSpec((1, 1, rows, 2 * HD), lambda b: (b, 0, 0, 0)),
+        ]
+        * chains,
         out_specs=pl.BlockSpec((BT, heads * HD), lambda b: (b, 0)),
         compiler_params=pltpu.CompilerParams(vmem_limit_bytes=40 * MIB),
         cost_estimate=pl.CostEstimate(
-            flops=8 * heads * tokens * (halo + BT) * HD,
-            bytes_accessed=4 * tokens * heads * HD * 4,
-            transcendentals=heads * tokens * (halo + BT),
+            flops=heads * tokens * HD, bytes_accessed=4 * tokens * heads * HD, transcendentals=0
         ),
-    )(q, lo_tok, k, v, m, acc)
+    )(q, lo_tok, k, v, *states)
 
 
 def out_kernel(ids_ref, *refs):
@@ -545,100 +550,29 @@
     depth = feat * N_TP
 
     wide = stream.astype(jnp.float32)
-    gain = lax.dynamic_slice_in_dim(norm_gain, z * feat, feat, 0).astype(jnp.float32)
-    scaled = (wide * gain[None, :]).astype(jnp.bfloat16)
-    arrivals, parts, places = gather_steps(scaled, z)
-    ids = jnp.concatenate([jnp.stack([chip, core]), places]).astype(jnp.int32)
-    step1, step2, step3 = (none_of(*pair) for pair in arrivals)
-    xs = []
-    for part in parts:
-        xs += [part, swap(part, 1)]
-
-    def halves(w, width, base):
-        mine = lax.dynamic_slice_in_dim(w, base + core * width, width, 1)
-        theirs = lax.dynamic_slice_in_dim(w, base + (1 - core) * width, width, 1)
-        return mine, swap(theirs, 1)
-
-    def plane(own, other, zero_other, zero_far):
-        own_x, own_y = swap(own, 2), swap(own, 4)
-        late = after(other, zero_other)
-        other_x, other_y = swap(late, 2), swap(late, 4)
-        far_own = swap(after(own_x, zero_far), 4)
-        far_other = swap(after(other_y, zero_far), 2)
-        return own, other, own_x, other_x, own_y, other_y, far_own, far_other
-
-    q_heads = w_query.shape[1] // HD // 2
-    wq_parts = plane(*halves(w_query, q_heads * HD, 0), step1, step2)
-    kv_old = jnp.stack([prefix_keys, prefix_values])
-    old_own = lax.dynamic_index_in_dim(kv_old, 2 * z + core, 1, keepdims=False)
-    old_other = swap(lax.dynamic_index_in_dim(kv_old, 2 * z + 1 - core, 1, keepdims=False), 1)
-    old_parts = plane(old_own, old_other, step1, step2)
-    span = old_own.shape[1]
-    kv = jnp.zeros((2, N_CTX * span, HD), jnp.bfloat16)
-    for index, part in enumerate(old_parts):
-        from_ctx = ((chip ^ (index // 2)) * 2 + (core ^ (index % 2))) * span
-        kv = lax.dynamic_update_slice(kv, part, (0, from_ctx, 0))
-
-    piece_rows = w_out.shape[0] // 4
-
-    def piece(q):
-        return lax.dynamic_slice_in_dim(w_out, q * piece_rows, piece_rows, 0)
-
-    to_x, to_y = swap(piece(chip ^ 1), 2), swap(piece(chip ^ 2), 4)
-    to_far = swap(after(piece(chip ^ 3), step1), 6)
-    by_chip = jnp.stack([piece(chip), to_x, to_y, to_far])
-
-    def of_chip(q):
-        return lax.dynamic_index_in_dim(by_chip, q ^ chip, 0, keepdims=False)
-
-    pieces = [of_chip(z)]
-    for r in (1, 2, 3):
-        pieces.append(
-            lax.ppermute(after(of_chip(z ^ r), step3), "tp", [(i, i ^ r) for i in range(N_TP)])
-        )
-    moved = none_of(*pieces[1:])
-    block = jnp.concatenate(pieces, axis=0)
-    half = block.shape[0] // 2
-    wo_x, wo_y = swap(block, 2), swap(block, 4)
-    wo_parts = (block, wo_x, wo_y, swap(wo_x[:half], 4), swap(wo_y[half:], 2))
-
-    def share(place):
-        return lax.dynamic_slice_in_dim(pending[0], jnp.clip(place, 0, N_TP - 1) * feat, feat, 1)
-
-    up = hop_up(after(share(z + 3), step1), (0,))
-    down = hop_down(after(share(z - 3), step1), (0,))
-    up = hop_up(after(share(z + 2) + up, step2), (0, 1))
-    down = hop_down(after(share(z - 2) + down, step2), (0, 1))
-    up = hop_up(after(share(z + 1) + up, moved), (0, 1, 2))
-    down = hop_down(after(share(z - 1) + down, moved), (0, 1, 2))
-    pending_share = (
-        share(z).astype(jnp.float32) + up.astype(jnp.float32) + down.astype(jnp.float32)
-    )
-
-    squares = jnp.sum(wide * wide, axis=1)[None, :]
-    for r in (1, 2):
-        squares = squares + lax.ppermute(squares, "tp", [(i, i ^ r) for i in range(N_TP)])
-    factor = lax.rsqrt(squares[0] * (1.0 / depth) + NORM_EPSILON)
-
     labels = jnp.arange(NTRAJ, dtype=jnp.int32)
-    counts = jnp.stack(
-        [
-            jnp.sum((prefix_segments[:, None] <= labels).astype(jnp.int32), axis=0),
-            jnp.sum((stretch_segments[:, None] < labels).astype(jnp.int32), axis=0),
-        ]
-    )
-    for bit in (1, 2, 4):
-        counts = counts + swap(counts, bit)
-
-    def of_chip_tokens(mine):
-        theirs = swap(mine, 1)
-        return jnp.where(
-            first, jnp.concatenate([mine, theirs], axis=0), jnp.concatenate([theirs, mine], axis=0)
-        )
-
-    factor = jnp.broadcast_to(of_chip_tokens(factor)[:, None], (chip_tok, 128))
-    segs = of_chip_tokens(stretch_segments)
-    onehot = (segs[:, None] == labels).astype(jnp.int32)
+    seen_counts = jnp.sum((prefix_segments[:, None] <= labels).astype(jnp.float32), axis=0)
+    start_counts = jnp.sum((stretch_segments[:, None] < labels).astype(jnp.float32), axis=0)
+    here = (jnp.arange(N_CTX) == c).astype(jnp.float32)[:, None]
+    lead = (z == 0).astype(jnp.float32)
+    sums = lax.psum(
+        jnp.concatenate(
+            [
+                (here * jnp.sum(wide * wide, axis=1)[None, :]).reshape(-1),
+                (here * stretch_segments.astype(jnp.float32)[None, :]).reshape(-1) * lead,
+                seen_counts * lead,
+                start_counts * lead,
+            ]
+        ),
+        ("ctx", "tp"),
+    )
+    all_tok = N_CTX * tok
+    squares = lax.dynamic_slice_in_dim(sums[:all_tok], chip * chip_tok, chip_tok, 0)
+    segs = lax.dynamic_slice_in_dim(sums[all_tok : 2 * all_tok], chip * chip_tok, chip_tok, 0)
+    counts = sums[2 * all_tok :].reshape(2, NTRAJ).astype(jnp.int32)
+    factor = lax.rsqrt(squares * (1.0 / depth) + NORM_EPSILON)
+    factor = jnp.broadcast_to(factor[:, None], (chip_tok, 128))
+    onehot = (segs.astype(jnp.int32)[:, None] == labels).astype(jnp.int32)
     n_tok = jnp.sum(onehot * counts[0], axis=1)
     lo_tok = jnp.sum(onehot * counts[1], axis=1) - chip * chip_tok + tok
     blocked = n_tok.reshape(chip_tok // BT, BT)
@@ -646,6 +580,119 @@
     n_wide = jnp.broadcast_to(n_tok[:, None], (chip_tok, 128))
     lo_wide = jnp.broadcast_to(lo_tok[:, None], (chip_tok, 128))
 
+    q_heads = w_query.shape[1] // HD // 2
+    q_cols = q_heads * HD
+    kv_old = jnp.stack([prefix_keys, prefix_values])
+
+    def query_cols(j):
+        return lax.dynamic_slice_in_dim(w_query, j * q_cols, q_cols, 1)
+
+    def old_rows(j):
+        head = lax.dynamic_index_in_dim(kv_old, 2 * z + j, 1, keepdims=False)
+        n = head.shape[1] // 2
+        return jnp.concatenate([head[0, :n], head[0, n:], head[1, :n], head[1, n:]], axis=1)
+
+    def kv_rows(j):
+        both = jnp.concatenate(
+            [lax.dynamic_slice_in_dim(w, (2 * z + j) * HD, HD, 1) for w in (w_key, w_value)], axis=1
+        )
+        n = both.shape[0] // 2
+        return jnp.concatenate([both[:n], both[n:]], axis=1)
+
+    def piece(q):
+        n = w_out.shape[0] // 4
+        rows = lax.dynamic_slice_in_dim(w_out, q * n, n, 0)
+        return jnp.concatenate([rows[:, :q_cols], rows[:, q_cols:]], axis=0)
+
+    def share(place):
+        return lax.dynamic_slice_in_dim(pending[0], jnp.clip(place, 0, N_TP - 1) * feat, feat, 1)
+
+    wq, old, wkv = query_cols(core), old_rows(core), kv_rows(core)
+    n_q, n_old = wq.shape[0], old.shape[0]
+    n_both = n_q + n_old
+
+    gain = lax.dynamic_slice_in_dim(norm_gain, z * feat, feat, 0).astype(jnp.float32)
+    scaled = (wide * gain[None, :]).astype(jnp.bfloat16)
+
+    every = (0, 1, 2)
+    u1, d1 = hop_up(scaled, every), hop_down(scaled, every)
+    x1 = swap(jnp.concatenate([wq, old, piece(chip ^ 1)], axis=0), 2)
+    y1 = swap(jnp.concatenate([wq, old, piece(chip ^ 2)], axis=0), 4)
+    given = swap(
+        jnp.concatenate([query_cols(1 - core), old_rows(1 - core), kv_rows(1 - core)], axis=0), 1
+    )
+    end1 = none_of(u1, d1, x1, y1, given)
+
+    u2 = hop_up(after(jnp.where(z == 0, share(z + 3), u1), end1), every)
+    d2 = hop_down(after(jnp.where(z == 3, share(z - 3), d1), end1), every)
+    far = piece(chip ^ 3)
+    n_far = far.shape[0] // 2
+    x2 = swap(after(jnp.concatenate([given[:n_both], far[:n_far]], axis=0), end1), 2)
+    y2 = swap(after(jnp.concatenate([given[:n_both], far[n_far:]], axis=0), end1), 4)
+    near = jnp.where(z < 2, d1, u1)
+    over1 = swap(after(jnp.concatenate([scaled, near], axis=0), end1), 1)
+    end2 = none_of(u2, d2, x2, y2, over1)
+
+    u3 = hop_up(
+        after(jnp.where(z == 2, u2, share(z + 2) + jnp.where(z == 1, u2, 0)), end2), every
+    )
+    d3 = hop_down(
+        after(jnp.where(z == 1, d2, share(z - 2) + jnp.where(z == 2, d2, 0)), end2), every
+    )
+    far_own = swap(after(jnp.concatenate([x1[:n_both], x2[n_both:]], axis=0), end2), 4)
+    far_other = swap(after(y2, end2), 2)
+    second = jnp.where(z < 2, d2, u2)
+    over2 = swap(after(second, end2), 1)
+    end3 = none_of(u3, d3, far_own, far_other, over2)
+
+    parts, places = line_parts(z, (u1, d1), (u2, d2), (u3, d3))
+    ids = jnp.concatenate([jnp.stack([chip, core]), places]).astype(jnp.int32)
+    third = parts[2]
+    xs = [scaled, over1, near, over1, second, over2, third, swap(third, 1)]
+    own_rows = (wq, given, x1, x2, y1, y2, far_own, far_other)
+    old_parts = (old,) + tuple(rows[n_q:n_both] for rows in own_rows[1:])
+    span = 2 * n_old
+    kv = jnp.zeros((2, N_CTX * span, HD), jnp.bfloat16)
+    for index, part in enumerate(old_parts):
+        from_ctx = ((chip ^ (index // 2)) * 2 + (core ^ (index % 2))) * span
+        cut = [part[:, i * HD : (i + 1) * HD] for i in range(4)]
+        part = jnp.stack(
+            [jnp.concatenate(cut[:2], axis=0), jnp.concatenate(cut[2:], axis=0)], axis=0
+        )
+        kv = lax.dynamic_update_slice(kv, part, (0, from_ctx, 0))
+
+    by_chip = jnp.stack(
+        [
+            piece(chip),
+            x1[n_both:],
+            y1[n_both:],
+            jnp.concatenate([far_own[n_both:], far_other[n_both:]], axis=0),
+        ]
+    )
+
+    def of_chip(q):
+        return lax.dynamic_index_in_dim(by_chip, q ^ chip, 0, keepdims=False)
+
+    swapped = none_of(xs[7]) + end3
+    pieces = [of_chip(z)]
+    for r in (1, 2, 3):
+        pieces.append(
+            lax.ppermute(after(of_chip(z ^ r), swapped), "tp", [(i, i ^ r) for i in range(N_TP)])
+        )
+    cores = [[2 * k + j for k in range(4)] for j in range(2)]
+    wkv_all = lax.all_gather(
+        after(jnp.concatenate([wkv, given[n_both:]], axis=0), end3),
+        "ctx",
+        axis_index_groups=cores,
+    )
+    n_kv = wkv.shape[0]
+    wkv_parts = []
+    for m in range(4):
+        block = lax.dynamic_index_in_dim(wkv_all, chip ^ m, 0, keepdims=False)
+        for rows in (block[:n_kv], block[n_kv:]):
+            cut = rows.shape[1] // 2
+            wkv_parts.append(jnp.concatenate([rows[:, :cut], rows[:, cut:]], axis=0))
+
     token_index = chip * chip_tok + jnp.arange(chip_tok, dtype=jnp.int32)
     positions = stretch_offset[0].astype(jnp.float32) + token_index.astype(jnp.float32)
     angles = positions[:, None] * inverse_freqs(HD)
@@ -654,26 +701,45 @@
     sinus = jnp.concatenate([-sinus, sinus], axis=1)
 
     scale = math.log2(math.e) / math.sqrt(HD)
-    q = project(ids, xs, wq_parts, factor, cosine, sinus, q_heads, q_heads, scale)
-    m, acc = attend_prefix(bounds, q, n_wide, kv)
-
-    mine_k, other_k = halves(w_key, HD, 2 * z * HD)
-    mine_v, other_v = halves(w_value, HD, 2 * z * HD)
-    wkv_parts = plane(
-        after(jnp.concatenate([mine_k, mine_v], axis=1), step3),
-        jnp.concatenate([other_k, other_v], axis=1),
-        step3,
-        step3,
-    )
-    kv_new = project(ids, xs, wkv_parts, factor, cosine, sinus, 2, 1, 1.0)
+    q = project(ids, xs, own_rows, factor, cosine, sinus, q_heads, q_heads, scale)
+    part_a = attend_prefix(bounds, q, 0, n_wide, kv)
+    end4 = none_of(part_a[0], *pieces[1:])
+    kv_new = project(ids, xs, wkv_parts, factor + end4, cosine, sinus, 2, 1, 1.0)
+    made = none_of(kv_new)
     before = lax.ppermute(kv_new[:, tok:], "ctx", [(i, i + 2) for i in range(N_CTX - 2)])
+    haloed = none_of(before)
+
+    u4 = hop_up(after(share(z + 1) + jnp.where(z == 0, 0, u3), made), every)
+    d4 = hop_down(after(share(z - 1) + jnp.where(z == 3, 0, d3), made), every)
+    n_piece = pieces[0].shape[0] // 2
+    block = after(
+        jnp.concatenate(
+            [jnp.concatenate([p[:n_piece], p[n_piece:]], axis=1) for p in pieces], axis=0
+        ),
+        haloed,
+    )
+    half = block.shape[0] // 2
+    wo_x, wo_y = swap(block, 2), swap(block, 4)
+    part_b = attend_prefix(bounds + haloed.astype(jnp.int32), q, 1, n_wide, kv)
     k_near = jnp.concatenate([before[0], kv_new[0]], axis=0)
     v_near = jnp.concatenate([before[1], kv_new[1]], axis=0)
-    attended = attend_new(q, lo_wide, k_near, v_near, m, acc)
-
-    _, heads_parts, _ = gather_steps(attended, z)
+    attended = attend_new(q, lo_wide, k_near, v_near, part_a + part_b)
+
+    attended = after(attended, none_of(u4, d4))
+    u1, d1 = hop_up(attended, every), hop_down(attended, every)
+    end6 = none_of(u1, d1, wo_x, wo_y)
+    u2, d2 = hop_up(after(u1, end6), (1, 2)), hop_down(after(d1, end6), (1, 2))
+    wo_parts = (
+        block,
+        wo_x,
+        wo_y,
+        swap(after(wo_x[:half], end6), 4),
+        swap(after(wo_y[half:], end6), 2),
+    )
+    u3, d3 = hop_up(u2, (2,)), hop_down(d2, (2,))
+    heads_parts, _ = line_parts(z, (u1, d1), (u2, d2), (u3, d3))
     hs = []
-    for part in heads_parts:
+    for part in (attended,) + heads_parts:
         hs += [part, swap(part, 1)]
     projected = out_project(ids, hs, wo_parts)
     mine = lax.dynamic_slice_in_dim(projected, core * tok, tok, 0)
@@ -683,6 +749,11 @@
         jnp.concatenate([mine, theirs], axis=1),
         jnp.concatenate([theirs, mine], axis=1),
     ).astype(jnp.float32)
+    pending_share = (
+        share(z).astype(jnp.float32)
+        + jnp.where(z == 0, 0, u4).astype(jnp.float32)
+        + jnp.where(z == 3, 0, d4).astype(jnp.float32)
+    )
     return (wide + (head_share + pending_share)).astype(jnp.bfloat16)
 
 

time: 501 us -> 516 us (1.030)
  the two profiles are of different devices: /device:TPU:6 before, /device:TPU:0 now
where the time goes in v3:
time: 516 us; the launch traced here: 508 us
  waiting for transfers between devices  160 us (31%)
  local copies, waits for them, and re-layouts  89 us (17%)
  other arithmetic  77.8 us (15%)
  starting transfers between devices  57.4 us (11%)
  Pallas kernels  49.3 us (10%)
  blocking collectives  38.6 us (7%)
  between operations  35.8 us (7%)
    ppermute x7, waiting for transfers between devices, hop_down(): return lax.ppermute(v, 'tp', [(N_TP - 1 - i, N_TP - 2 - i) for i in pairs])  59.2 us
    ppermute x7, waiting for transfers between devices, hop_up(): return lax.ppermute(v, 'tp', [(i, i + 1) for i in pairs])  49.2 us
    unnamed x183, local copies, waits for them, and re-layouts  43.9 us
    psum x1, blocking collectives, per_device(): lax.psum(jnp.concatenate([(here * jnp.sum(wide * wide, axis=1)[None, :])....  38.6 us
    add x15, other arithmetic, after(): return x + zero.astype(x.dtype)  38.3 us
    ppermute x19, waiting for transfers between devices, swap(): return lax.ppermute(x, 'ctx', [(c, c ^ bit) for c in range(N_CTX)])  29.7 us
    ppermute x7, starting transfers between devices, hop_up(): return lax.ppermute(v, 'tp', [(i, i + 1) for i in pairs])  25.8 us
    ppermute x3, waiting for transfers between devices, per_device(): lax.ppermute(after(of_chip(z ^ r), swapped), 'tp', [(i, i ^ r) for i in r...  21.4 us
  transfers between devices with their start and end apart: 38, of which 13 were waited for; matrix products, arithmetic and copies ran while one was open for 23% of the time, Pallas kernels for 6%

profile of v3, /device:TPU:0, one launch (start us, length us, event | category | flops | bytes accessed | tf_op | source)
XLA Modules:
  0.0 507.5 jit_solution(2432756298567942657)
XLA Ops:
  10.5 7.3 %fusion.12 = bf16[1920,512]{1,0:T(8,128)(2,1)} fusion(bf16[1024,128]{1,0:T(8,128)(2,1)S(1)} %get-tuple-element.54, bf16[1024,128]{1,0:T(8,128)(2,1)S(1)} %get-tuple-element.140, bf16[512,256]{1,0:T(8,128)(2,1)S(1)} %fusion.28, bf16[384,128]{1,0:T(8,128)(2,1)S(1)} %get-tuple-element.120, bf16[384,128]{1,0:T(8,128)(2,1)S(1)} %get-tuple-element.121, ...), kind=kLoop, calls=%fused_computation.25 | loop fusion | flops 22609920 | bytes 4194304 | tf_op jit(solution)/shard_map/concatenate | solution.py:622
  20.9 7.4 %pad_maximum_fusion.2 = (bf16[1920,512]{1,0:T(8,128)(2,1)}, bf16[1920,512]{1,0:T(8,128)(2,1)}) fusion(bf16[256,512]{1,0:T(8,128)(2,1)S(1)} %get-tuple-element.47, bf16[256,512]{1,0:T(8,128)(2,1)S(1)} %get-tuple-element.45, bf16[384,128]{1,0:T(8,128)(2,1)S(1)} %get-tuple-element.144, bf16[384,128]{1,0:T(8,128)(2,1)S(1)} %get-tuple-element.143, ...), kind=kLoop, calls=%fused_computation.28 | loop fusion | flops 18677760 | bytes 6422528 | tf_op jit(solution)/shard_map/concatenate | solution.py:620
  35.0 4.6 collective-permute-start.1
  41.9 30.3 %collective-permute-done.1 = bf16[384,2048]{1,0:T(8,128)(2,1)} collective-permute-done((bf16[384,2048]{1,0:T(8,128)(2,1)S(1)}, bf16[384,2048]{1,0:T(8,128)(2,1)}, u32[]{:S(2)}, u32[]{:S(2)}) %collective-permute-start.1) | collective-permute-done | bytes 1572896 | tf_op jit(solution)/shard_map/ppermute | solution.py:179
  90.9 5.1 %fusion.20 = (bf16[384,2048]{1,0:T(8,128)(2,1)}, bf16[384,2048]{1,0:T(8,128)(2,1)}, bf16[384,2048]{1,0:T(8,128)(2,1)S(1)}) fusion(bf16[384,2048]{1,0:T(8,128)(2,1)} %collective-permute-done, bf16[1,384,8192]{2,1,0:T(8,128)(2,1)S(1)} %bitcast.209, s32[]{:T(128)S(6)} %select_n.287, pred[]{:T(512)S(6)} %eq.29, bf16[]{:T(256)} %bitcast.18, ...), kind=kLoop, calls=%fused_computation.46 | loop fusion | flops 7864320 | bytes 11010061 | tf_op jit(solution)/shard_map/add | solution.py:194
  98.9 38.6 %psum.7 = f32[6176]{0:T(1024)S(1)} all-reduce(f32[6176]{0:T(1024)S(1)} %concatenate.182), channel_id=1, replica_groups=mesh['ctx'=8,'tp'=4] {'ctx','tp'}, use_global_device_ids=true, to_apply=%region_3.4 | all-reduce | flops 6176 | bytes 49408 | tf_op jit(solution)/shard_map/psum | solution.py:558
  144.1 6.3 %collective-permute-start.7 = (bf16[384,2048]{1,0:T(8,128)(2,1)}, bf16[384,2048]{1,0:T(8,128)(2,1)}, u32[]{:S(2)}, u32[]{:S(2)}) collective-permute-start(bf16[384,2048]{1,0:T(8,128)(2,1)} %get-tuple-element.24), channel_id=1, source_target_pairs={{0,1},{1,2},{2,3},{4,5},{5,6},{6,7},{8,9},{9,10},{10,11},{12,13},{... | collective-permute-start | bytes 4718600 | tf_op jit(solution)/shard_map/ppermute | solution.py:179
  155.7 24.1 %collective-permute-done.6 = bf16[384,2048]{1,0:T(8,128)(2,1)} collective-permute-done((bf16[384,2048]{1,0:T(8,128)(2,1)}, bf16[384,2048]{1,0:T(8,128)(2,1)}, u32[]{:S(2)}, u32[]{:S(2)}) %collective-permute-start.6) | collective-permute-done | bytes 1572896 | tf_op jit(solution)/shard_map/ppermute | solution.py:183
  204.1 4.8 fusion.16
  208.9 4.5 collective-permute-start.12
  224.3 18.9 %collective-permute-done.12 = bf16[384,2048]{1,0:T(8,128)(2,1)} collective-permute-done((bf16[384,2048]{1,0:T(8,128)(2,1)}, bf16[384,2048]{1,0:T(8,128)(2,1)}, u32[]{:S(2)}, u32[]{:S(2)}) %collective-permute-start.12) | collective-permute-done | bytes 1572896 | tf_op jit(solution)/shard_map/ppermute | solution.py:179
  286.3 9.9 %shard_map.118.q_ref = bf16[4,768,128]{2,1,0:T(8,128)(2,1)S(1)} custom-call(s32[6]{0:T(128)S(1)} %concatenate.170.ids_ref, bf16[384,2048]{1,0:T(8,128)(2,1)S(1)} %copy-done.4, bf16[768,2048]{1,0:T(8,128)(2,1)} %collective-permute-done.5.refs_1_.refs_3_, bf16[384,2048]{1,0:T(8,128)(2,1)S(1)} %copy-done.1, ...), custom_call_target="tpu_custom_call" | custom-call | flops 6442450944 | bytes 20971520 | tf_op jit(solution)/shard_map/pallas_call | solution.py:275
  296.4 7.7 %shard_map.119 = (f32[3,1,512,128]{3,2,1,0:T(8,128)S(1)}, f32[3,1,512,256]{3,2,1,0:T(8,128)S(1)}) custom-call(s32[2,3]{1,0:T(2,128)S(1)} %pad_add_fusion.bound_ref, bf16[4,768,128]{2,1,0:T(8,128)(2,1)S(1)} %shard_map.118.q_ref, s32[768,128]{1,0:T(8,128)S(1)} %broadcast_in_dim.21.n_ref, bf16[2,6144,128]{2,1,0:T(8,128)(2,1)S(1)} %maximum_dynamic-update-slice_fusion.7.kv_ref), custom_call_target="tpu_custom_call" | custom-call | flops 196608 | bytes 3145728 | tf_op jit(solution)/shard_map/pallas_call | solution.py:370
  307.0 21.4 %collective-permute-done.17 = bf16[512,512]{1,0:T(8,128)(2,1)S(1)} collective-permute-done((bf16[512,512]{1,0:T(8,128)(2,1)S(1)}, bf16[512,512]{1,0:T(8,128)(2,1)S(1)}, u32[]{:S(2)}, u32[]{:S(2)}) %collective-permute-start.17) | collective-permute-done | bytes 524320 | tf_op jit(solution)/shard_map/ppermute | solution.py:680
  340.6 9.5 %shard_map.120 = bf16[2,768,128]{2,1,0:T(8,128)(2,1)S(1)} custom-call(s32[6]{0:T(128)S(1)} %concatenate.170.ids_ref, bf16[384,2048]{1,0:T(8,128)(2,1)S(1)} %copy-done.5, bf16[768,2048]{1,0:T(8,128)(2,1)} %collective-permute-done.5.refs_1_.refs_3_, bf16[384,2048]{1,0:T(8,128)(2,1)S(1)} %copy-done.2, bf16[768,2048]{1,0:T(8,128)(2,1)} %collective-permute-done.5.refs_1_.refs_3_, ...), custom_call_target="tpu_custom_call" | custom-call | flops 3221225472 | bytes 16777216 | tf_op jit(solution)/shard_map/pallas_call | solution.py:275
  359.3 5.1 %collective-permute-start.20 = (bf16[384,2048]{1,0:T(8,128)(2,1)S(1)}, bf16[384,2048]{1,0:T(8,128)(2,1)S(1)}, u32[]{:S(2)}, u32[]{:S(2)}) collective-permute-start(bf16[384,2048]{1,0:T(8,128)(2,1)S(1)} %get-tuple-element.20), channel_id=1, source_target_pairs={{0,1},{1,2},{2,3},{4,5},{5,6},{6,7},{8,9},{9,10},{10,11},{12,13},{... | collective-permute-start | bytes 4718600 | tf_op jit(solution)/shard_map/ppermute | solution.py:179
  365.8 12.6 %maximum_add_fusion.1.refs_8_ = bf16[1024,1024]{1,0:T(8,128)(2,1)S(1)} fusion(bf16[256,512]{1,0:T(8,128)(2,1)S(1)} %copy-done.52, bf16[256,512]{1,0:T(8,128)(2,1)S(1)} %copy-done.51, bf16[256,512]{1,0:T(8,128)(2,1)S(1)} %copy-done.54, bf16[256,512]{1,0:T(8,128)(2,1)S(1)} %copy-done.53, bf16[256,512]{1,0:T(8,128)(2,1)S(1)} %get-tuple-element.96, ...), kind=kLoop, calls=%fused_computation.22 | loop fusion | flops 18874368 | bytes 4194306 | tf_op jit(solution)/shard_map/add | solution.py:194
  380.3 7.7 %shard_map.121 = (f32[3,1,512,128]{3,2,1,0:T(8,128)S(1)}, f32[3,1,512,256]{3,2,1,0:T(8,128)S(1)}) custom-call(s32[2,3]{1,0:T(2,128)S(1)} %broadcast_add_fusion.6.bound_ref, bf16[4,768,128]{2,1,0:T(8,128)(2,1)S(1)} %copy-done.12, s32[768,128]{1,0:T(8,128)S(1)} %copy-done.20, bf16[2,6144,128]{2,1,0:T(8,128)(2,1)S(1)} %maximum_dynamic-update-slice_fusion.7.kv_ref), custom_call_target="tpu_custom_call" | custom-call | flops 196608 | bytes 3145728 | tf_op jit(solution)/shard_map/pallas_call | solution.py:370
  388.3 4.5 shard_map.122
  404.4 20.3 %collective-permute-done.27.refs_10_ = bf16[1024,1024]{1,0:T(8,128)(2,1)S(1)} collective-permute-done((bf16[1024,1024]{1,0:T(8,128)(2,1)S(1)}, bf16[1024,1024]{1,0:T(8,128)(2,1)S(1)}, u32[]{:S(2)}, u32[]{:S(2)}) %collective-permute-start.27) | collective-permute-done | bytes 2097184 | tf_op jit(solution)/shard_map/ppermute | solution.py:175
  433.3 17.0 %collective-permute-done.28 = bf16[768,512]{1,0:T(8,128)(2,1)S(1)} collective-permute-done((bf16[768,512]{1,0:T(8,128)(2,1)S(1)}, bf16[768,512]{1,0:T(8,128)(2,1)S(1)}, u32[]{:S(2)}, u32[]{:S(2)}) %collective-permute-start.28) | collective-permute-done | bytes 786464 | tf_op jit(solution)/shard_map/ppermute | solution.py:183
  457.5 10.9 %collective-permute-done.31 = bf16[768,512]{1,0:T(8,128)(2,1)S(1)} collective-permute-done((bf16[768,512]{1,0:T(8,128)(2,1)S(1)}, bf16[768,512]{1,0:T(8,128)(2,1)S(1)}, u32[]{:S(2)}, u32[]{:S(2)}) %collective-permute-start.31) | collective-permute-done | bytes 786464 | tf_op jit(solution)/shard_map/ppermute | solution.py:183
  481.9 10.0 %shard_map.123 = bf16[768,1024]{1,0:T(8,128)(2,1)S(1)} custom-call(s32[6]{0:T(128)S(1)} %concatenate.170.ids_ref, bf16[768,512]{1,0:T(8,128)(2,1)S(1)} %copy-done.28, bf16[768,512]{1,0:T(8,128)(2,1)S(1)} %copy-done.30, bf16[768,512]{1,0:T(8,128)(2,1)} %get-tuple-element.88.refs_2_, bf16[768,512]{1,0:T(8,128)(2,1)} %collective-permute-done.25.refs_3_, ...), custom_call_target="tpu_custom_call" | custom-call | flops 6442450944 | bytes 14680064 | tf_op jit(solution)/shard_map/pallas_call | solution.py:510
  495.8 4.6 fusion.5
  (405 shorter events, 178.5 us)
Async XLA Ops:
  6.5 328.3 %all-gather.2.cloned.1.call-start = ((), (), s32[]{:S(2)}) async-start(), calls=%async_computation | async-start | bytes 5242880 | tf_op jit(solution)/shard_map/all_gather | solution.py:683
  17.8 62.7 %collective-permute-start.4 = (bf16[1920,512]{1,0:T(8,128)(2,1)}, bf16[1920,512]{1,0:T(8,128)(2,1)S(1)}, u32[]{:S(2)}, u32[]{:S(2)}) collective-permute-start(bf16[1920,512]{1,0:T(8,128)(2,1)} %fusion.12), channel_id=1, source_target_pairs={{0,4},{4,0},{8,12},{12,8},{16,20},{20,16},{24,28},{28,24},{1,5},{5... | collective-permute-start | bytes 5898248 | tf_op jit(solution)/shard_map/ppermute | solution.py:175
  28.3 54.9 %collective-permute-start.3 = (bf16[1920,512]{1,0:T(8,128)(2,1)}, bf16[1920,512]{1,0:T(8,128)(2,1)}, u32[]{:S(2)}, u32[]{:S(2)}) collective-permute-start(bf16[1920,512]{1,0:T(8,128)(2,1)} %get-tuple-element.93), channel_id=1, source_target_pairs={{0,16},{4,20},{8,24},{12,28},{16,0},{20,4},{24,8},{28,12},{1,17},{... | collective-permute-start | bytes 5898248 | tf_op jit(solution)/shard_map/ppermute | solution.py:175
  30.8 56.3 %collective-permute-start.2 = (bf16[1920,512]{1,0:T(8,128)(2,1)}, bf16[1920,512]{1,0:T(8,128)(2,1)}, u32[]{:S(2)}, u32[]{:S(2)}) collective-permute-start(bf16[1920,512]{1,0:T(8,128)(2,1)} %get-tuple-element.94), channel_id=1, source_target_pairs={{0,8},{4,12},{8,0},{12,4},{16,24},{20,28},{24,16},{28,20},{1,9},{5... | collective-permute-start | bytes 5898248 | tf_op jit(solution)/shard_map/ppermute | solution.py:175
  35.0 37.2 %collective-permute-start.1 = (bf16[384,2048]{1,0:T(8,128)(2,1)S(1)}, bf16[384,2048]{1,0:T(8,128)(2,1)}, u32[]{:S(2)}, u32[]{:S(2)}) collective-permute-start(bf16[384,2048]{1,0:T(8,128)(2,1)S(1)} %get-tuple-element.90.refs_0_), channel_id=1, source_target_pairs={{0,1},{1,2},{2,3},{4,5},{5,6},{6,7},{8,9},{9,10},{10,11},{12,13},{... | collective-permute-start | bytes 4718600 | tf_op jit(solution)/shard_map/ppermute | solution.py:179
  39.6 38.0 %collective-permute-start = (bf16[384,2048]{1,0:T(8,128)(2,1)S(1)}, bf16[384,2048]{1,0:T(8,128)(2,1)}, u32[]{:S(2)}, u32[]{:S(2)}) collective-permute-start(bf16[384,2048]{1,0:T(8,128)(2,1)S(1)} %get-tuple-element.90.refs_0_), channel_id=1, source_target_pairs={{3,2},{2,1},{1,0},{7,6},{6,5},{5,4},{11,10},{10,9},{9,8},{15,14},{... | collective-permute-start | bytes 4718600 | tf_op jit(solution)/shard_map/ppermute | solution.py:183
  98.5 95.9 %collective-permute-start.5 = (bf16[768,2048]{1,0:T(8,128)(2,1)}, bf16[768,2048]{1,0:T(8,128)(2,1)}, u32[]{:S(2)}, u32[]{:S(2)}) collective-permute-start(bf16[768,2048]{1,0:T(8,128)(2,1)} %maximum_add_fusion), channel_id=1, source_target_pairs={{0,4},{4,0},{8,12},{12,8},{16,20},{20,16},{24,28},{28,24},{1,5},{5... | collective-permute-start | bytes 9437192 | tf_op jit(solution)/shard_map/ppermute | solution.py:175
  139.9 46.1 %collective-permute-start.9 = (bf16[1664,512]{1,0:T(8,128)(2,1)}, bf16[1664,512]{1,0:T(8,128)(2,1)}, u32[]{:S(2)}, u32[]{:S(2)}) collective-permute-start(bf16[1664,512]{1,0:T(8,128)(2,1)} %get-tuple-element.91), channel_id=1, source_target_pairs={{0,16},{4,20},{8,24},{12,28},{16,0},{20,4},{24,8},{28,12},{1,17},{... | collective-permute-start | bytes 5111816 | tf_op jit(solution)/shard_map/ppermute | solution.py:175
  142.2 47.5 %collective-permute-start.8 = (bf16[1664,512]{1,0:T(8,128)(2,1)}, bf16[1664,512]{1,0:T(8,128)(2,1)}, u32[]{:S(2)}, u32[]{:S(2)}) collective-permute-start(bf16[1664,512]{1,0:T(8,128)(2,1)} %get-tuple-element.92), channel_id=1, source_target_pairs={{0,8},{4,12},{8,0},{12,4},{16,24},{20,28},{24,16},{28,20},{1,9},{5... | collective-permute-start | bytes 5111816 | tf_op jit(solution)/shard_map/ppermute | solution.py:175
  142.8 37.1 %collective-permute-start.6 = (bf16[384,2048]{1,0:T(8,128)(2,1)}, bf16[384,2048]{1,0:T(8,128)(2,1)}, u32[]{:S(2)}, u32[]{:S(2)}) collective-permute-start(bf16[384,2048]{1,0:T(8,128)(2,1)} %get-tuple-element.23), channel_id=1, source_target_pairs={{3,2},{2,1},{1,0},{7,6},{6,5},{5,4},{11,10},{10,9},{9,8},{15,14},{... | collective-permute-start | bytes 4718600 | tf_op jit(solution)/shard_map/ppermute | solution.py:183
  144.1 38.8 %collective-permute-start.7 = (bf16[384,2048]{1,0:T(8,128)(2,1)}, bf16[384,2048]{1,0:T(8,128)(2,1)}, u32[]{:S(2)}, u32[]{:S(2)}) collective-permute-start(bf16[384,2048]{1,0:T(8,128)(2,1)} %get-tuple-element.24), channel_id=1, source_target_pairs={{0,1},{1,2},{2,3},{4,5},{5,6},{6,7},{8,9},{9,10},{10,11},{12,13},{... | collective-permute-start | bytes 4718600 | tf_op jit(solution)/shard_map/ppermute | solution.py:179
  201.4 53.1 %collective-permute-start.15 = (bf16[1664,512]{1,0:T(8,128)(2,1)}, bf16[1664,512]{1,0:T(8,128)(2,1)}, u32[]{:S(2)}, u32[]{:S(2)}) collective-permute-start(bf16[1664,512]{1,0:T(8,128)(2,1)} %broadcast_add_fusion), channel_id=1, source_target_pairs={{0,8},{4,12},{8,0},{12,4},{16,24},{20,28},{24,16},{28,20},{1,9},{5... | collective-permute-start | bytes 5111816 | tf_op jit(solution)/shard_map/ppermute | solution.py:175
  203.4 54.6 %collective-permute-start.14 = (bf16[1664,512]{1,0:T(8,128)(2,1)}, bf16[1664,512]{1,0:T(8,128)(2,1)}, u32[]{:S(2)}, u32[]{:S(2)}) collective-permute-start(bf16[1664,512]{1,0:T(8,128)(2,1)} %maximum_add_fusion.4), channel_id=1, source_target_pairs={{0,16},{4,20},{8,24},{12,28},{16,0},{20,4},{24,8},{28,12},{1,17},{... | collective-permute-start | bytes 5111816 | tf_op jit(solution)/shard_map/ppermute | solution.py:175
  208.9 34.2 %collective-permute-start.12 = (bf16[384,2048]{1,0:T(8,128)(2,1)}, bf16[384,2048]{1,0:T(8,128)(2,1)}, u32[]{:S(2)}, u32[]{:S(2)}) collective-permute-start(bf16[384,2048]{1,0:T(8,128)(2,1)} %get-tuple-element.21), channel_id=1, source_target_pairs={{0,1},{1,2},{2,3},{4,5},{5,6},{6,7},{8,9},{9,10},{10,11},{12,13},{... | collective-permute-start | bytes 4718600 | tf_op jit(solution)/shard_map/ppermute | solution.py:179
  213.4 35.0 %collective-permute-start.11 = (bf16[384,2048]{1,0:T(8,128)(2,1)}, bf16[384,2048]{1,0:T(8,128)(2,1)}, u32[]{:S(2)}, u32[]{:S(2)}) collective-permute-start(bf16[384,2048]{1,0:T(8,128)(2,1)} %get-tuple-element.22), channel_id=1, source_target_pairs={{3,2},{2,1},{1,0},{7,6},{6,5},{5,4},{11,10},{10,9},{9,8},{15,14},{... | collective-permute-start | bytes 4718600 | tf_op jit(solution)/shard_map/ppermute | solution.py:183
  214.9 36.6 %collective-permute-start.10 = (bf16[384,2048]{1,0:T(8,128)(2,1)}, bf16[384,2048]{1,0:T(8,128)(2,1)}, u32[]{:S(2)}, u32[]{:S(2)}) collective-permute-start(bf16[384,2048]{1,0:T(8,128)(2,1)} %get-tuple-element.34), channel_id=1, source_target_pairs={{0,4},{4,0},{8,12},{12,8},{16,20},{20,16},{24,28},{28,24},{1,5},{5... | collective-permute-start | bytes 4718600 | tf_op jit(solution)/shard_map/ppermute | solution.py:175
  283.6 44.8 %collective-permute-start.17 = (bf16[512,512]{1,0:T(8,128)(2,1)S(1)}, bf16[512,512]{1,0:T(8,128)(2,1)S(1)}, u32[]{:S(2)}, u32[]{:S(2)}) collective-permute-start(bf16[512,512]{1,0:T(8,128)(2,1)S(1)} %get-tuple-element.41), channel_id=1, source_target_pairs={{0,2},{1,3},{2,0},{3,1},{4,6},{5,7},{6,4},{7,5},{8,10},{9,11},{10,... | collective-permute-start | bytes 1572872 | tf_op jit(solution)/shard_map/ppermute | solution.py:680
  283.6 46.3 %collective-permute-start.16 = (bf16[512,512]{1,0:T(8,128)(2,1)S(1)}, bf16[512,512]{1,0:T(8,128)(2,1)S(1)}, u32[]{:S(2)}, u32[]{:S(2)}) collective-permute-start(bf16[512,512]{1,0:T(8,128)(2,1)S(1)} %get-tuple-element.42), channel_id=1, source_target_pairs={{0,1},{1,0},{2,3},{3,2},{4,5},{5,4},{6,7},{7,6},{8,9},{9,8},{10,11... | collective-permute-start | bytes 1572872 | tf_op jit(solution)/shard_map/ppermute | solution.py:680
  358.0 37.4 %collective-permute-start.21 = (bf16[384,2048]{1,0:T(8,128)(2,1)S(1)}, bf16[384,2048]{1,0:T(8,128)(2,1)S(1)}, u32[]{:S(2)}, u32[]{:S(2)}) collective-permute-start(bf16[384,2048]{1,0:T(8,128)(2,1)S(1)} %get-tuple-element.19), channel_id=1, source_target_pairs={{3,2},{2,1},{1,0},{7,6},{6,5},{5,4},{11,10},{10,9},{9,8},{15,14},{... | collective-permute-start | bytes 4718600 | tf_op jit(solution)/shard_map/ppermute | solution.py:183
  359.3 37.9 %collective-permute-start.20 = (bf16[384,2048]{1,0:T(8,128)(2,1)S(1)}, bf16[384,2048]{1,0:T(8,128)(2,1)S(1)}, u32[]{:S(2)}, u32[]{:S(2)}) collective-permute-start(bf16[384,2048]{1,0:T(8,128)(2,1)S(1)} %get-tuple-element.20), channel_id=1, source_target_pairs={{0,1},{1,2},{2,3},{4,5},{5,6},{6,7},{8,9},{9,10},{10,11},{12,13},{... | collective-permute-start | bytes 4718600 | tf_op jit(solution)/shard_map/ppermute | solution.py:179
  378.4 46.3 %collective-permute-start.27 = (bf16[1024,1024]{1,0:T(8,128)(2,1)S(1)}, bf16[1024,1024]{1,0:T(8,128)(2,1)S(1)}, u32[]{:S(2)}, u32[]{:S(2)}) collective-permute-start(bf16[1024,1024]{1,0:T(8,128)(2,1)S(1)} %maximum_add_fusion.1.refs_8_), channel_id=1, source_target_pairs={{0,16},{4,20},{8,24},{12,28},{16,0},{20,4},{24,8},{28,12},{1,17},{... | collective-permute-start | bytes 6291464 | tf_op jit(solution)/shard_map/ppermute | solution.py:175
  380.2 46.2 %collective-permute-start.26 = (bf16[1024,1024]{1,0:T(8,128)(2,1)S(1)}, bf16[1024,1024]{1,0:T(8,128)(2,1)S(1)}, u32[]{:S(2)}, u32[]{:S(2)}) collective-permute-start(bf16[1024,1024]{1,0:T(8,128)(2,1)S(1)} %maximum_add_fusion.1.refs_8_), channel_id=1, source_target_pairs={{0,8},{4,12},{8,0},{12,4},{16,24},{20,28},{24,16},{28,20},{1,9},{5... | collective-permute-start | bytes 6291464 | tf_op jit(solution)/shard_map/ppermute | solution.py:175
  399.1 29.1 %collective-permute-start.24 = (bf16[768,512]{1,0:T(8,128)(2,1)S(1)}, bf16[768,512]{1,0:T(8,128)(2,1)S(1)}, u32[]{:S(2)}, u32[]{:S(2)}) collective-permute-start(bf16[768,512]{1,0:T(8,128)(2,1)S(1)} %broadcast_add_fusion.4.refs_0_), channel_id=1, source_target_pairs={{0,1},{1,2},{2,3},{4,5},{5,6},{6,7},{8,9},{9,10},{10,11},{12,13},{... | collective-permute-start | bytes 2359304 | tf_op jit(solution)/shard_map/ppermute | solution.py:179
  433.2 37.2 %collective-permute-start.22 = (bf16[768,512]{1,0:T(8,128)(2,1)S(1)}, bf16[768,512]{1,0:T(8,128)(2,1)S(1)}, u32[]{:S(2)}, u32[]{:S(2)}) collective-permute-start(bf16[768,512]{1,0:T(8,128)(2,1)S(1)} %broadcast_add_fusion.4.refs_0_), channel_id=1, source_target_pairs={{0,4},{4,0},{8,12},{12,8},{16,20},{20,16},{24,28},{28,24},{1,5},{5... | collective-permute-start | bytes 2359304 | tf_op jit(solution)/shard_map/ppermute | solution.py:175
  (93 other events, 1117.6 us)
Sparse Core Ops, SparseCore 0:
  262.9 52.5 all-gather.1
